TPU v7x, 32 devices: a whole 2x2x4 slice. The times are simulated.
32 devices in a mesh: section: 2 (over x), dp: 4 (over z), mp: 4 (over y, core).
Axes of the slice: x: 2, y: 2, z: 4, core: 2. Of those that a mesh axis runs over, the one named last changes fastest.
Arguments:
- embeddings: bfloat16 [2, 12, 1024, 512], P('section', 'dp', 'mp'), may hold values from -6 to 6
- src_len: int32 [12, 4], P('dp'), may hold values from 1 to 512, 896 in all within a row
- tgt_len: int32 [12, 4], P('dp'), may hold values from 1 to 512, 896 in all within a row
- attn_in: bfloat16 [2, 3, 512, 512], P('section', None, None, 'mp'), may hold values from -0.25 to 0.25
- attn_out: bfloat16 [2, 512, 512], P('section', 'mp'), may hold values from -1 to 1
- ffn_in: bfloat16 [2, 512, 2048], P('section', None, 'mp'), may hold values from -0.25 to 0.25
- ffn_out: bfloat16 [2, 2048, 512], P('section', 'mp'), may hold values from -0.125 to 0.125
- cross_a: bfloat16 [2, 512, 512], P('section', None, 'mp'), may hold values from -0.25 to 0.25
- cross_b: bfloat16 [2, 512, 512], P('section', None, 'mp'), may hold values from -1 to 1
- norm_gain: float32 [2, 2, 512], P('section'), may hold values from 0.5 to 1.5
- norm_bias: float32 [2, 2, 512], P('section'), may hold values from -1.8 to 1.8
- cross_gain: float32 [512], replicated, may hold values from 0.5 to 1.5
- cross_bias: float32 [512], replicated, may hold values from -1.8 to 1.8
- cotangent: bfloat16 [12, 1024, 512], P('dp', 'mp'), may hold values from -6 to 6
Outputs:
- layer_out: bfloat16 [2, 12, 1024, 512], P('section', 'dp', 'mp')
- input_grad: float32 [2, 12, 1024, 512], P('section', 'dp', 'mp')
- grad_attn_in: float32 [2, 3, 512, 512], P('section', None, None, 'mp')
- grad_attn_out: float32 [2, 512, 512], P('section', 'mp')
- grad_ffn_in: float32 [2, 512, 2048], P('section', None, 'mp')
- grad_ffn_out: float32 [2, 2048, 512], P('section', 'mp')
- grad_cross_a: float32 [2, 512, 512], P('section', None, 'mp')
- grad_cross_b: float32 [2, 512, 512], P('section', None, 'mp')
- grad_norm_gain: float32 [2, 2, 512], P('section')
- grad_norm_bias: float32 [2, 2, 512], P('section')
- grad_cross_gain: float32 [512], replicated
- grad_cross_bias: float32 [512], replicated
Inputs may be any that keep to these rules, and one draw needn't show every extreme that they name: `src_len`: each row lists the sentences packed into one pack in order; a row sums to 896 and its largest entry is 512; the remaining slots are padding. `tgt_len`: each row lists the sentences packed into one pack in order; a row sums to 896 and its largest entry is 512; target sentence j translates source sentence j of the same pack.
All inputs are finite; a program needn't handle non-finite values.
Results may differ from a plain program's by a relative error of at most 0.035.
Values may be sent and summed in bfloat16 or wider, within the bound.
No kernel may reach another device: no remote copies, remote signals or barrier semaphores. Data moves between devices by JAX's collectives and lax.ppermute only.
A program may use at most 256 MiB of HBM per device.

v0:
```python
import jax
import jax.numpy as jnp
from jax import lax
from jax.sharding import PartitionSpec as P

HD = 64


EPS = 1e-05
NEG = -1000000000.0


def passed_along(value, axis, steps):
    count = lax.axis_size(axis)
    initial, last = (max(0, -steps), min(count, count - steps))
    return lax.ppermute(value, axis, [(source, source + steps) for source in range(initial, last)])


def shortened(x):
    return jax.tree.map(lambda a: a.astype(jnp.bfloat16) if a.dtype == jnp.float32 else a, x)


def segment_ids(lengths, count):
    ends = jnp.cumsum(lengths)
    position = jnp.arange(count, dtype=jnp.int32)
    return jnp.sum((position[:, None] >= ends[None, :]).astype(jnp.int32), axis=1)


def norm_rows(total, gain, shift_bias):
    center = jnp.mean(total, axis=-1, keepdims=True)
    centred = total - center
    inverse = lax.rsqrt(jnp.mean(centred * centred, axis=-1, keepdims=True) + EPS)
    scaled = centred * inverse
    return (scaled * gain + shift_bias, scaled, inverse)


def norm_back(grad, scaled, inverse, gain):
    inner = grad * gain
    first_mean = jnp.mean(inner, axis=-1, keepdims=True)
    second_mean = jnp.mean(inner * scaled, axis=-1, keepdims=True)
    return (
        inverse * (inner - first_mean - scaled * second_mean),
        jnp.sum(grad * scaled, axis=0),
        jnp.sum(grad, axis=0),
    )


def widen(rows):
    return lax.all_gather(rows, "mp", axis=0, tiled=True)


def narrow(partial_value):
    return lax.psum_scatter(
        partial_value.astype(jnp.bfloat16), "mp", scatter_dimension=0, tiled=True
    ).astype(jnp.float32)


def plain_dot(left, right):
    return jnp.dot(left, right, preferred_element_type=jnp.float32)


def left_dot(left, right):
    return lax.dot_general(
        left, right, (((0,), (0,)), ((), ())), preferred_element_type=jnp.float32
    )


def right_dot(left, right):
    return lax.dot_general(
        left, right, (((1,), (1,)), ((), ())), preferred_element_type=jnp.float32
    )


def split_heads(matrix):
    return matrix.reshape(matrix.shape[0], -1, HD)


def softmax_block(query_block, key_heads, query_seg, key_seg, query_pos, key_pos, causal, scale):
    scores = (
        jnp.einsum("qhd,khd->hqk", query_block, key_heads, preferred_element_type=jnp.float32)
        * scale
    )
    allowed = (query_seg[:, None] == key_seg[None, :]) & (
        (key_pos[None, :] <= query_pos[:, None]) | jnp.logical_not(causal)
    )
    scores = jnp.where(allowed[None], scores, NEG)
    top_score = jnp.max(scores, axis=-1, keepdims=True)
    raised = jnp.exp(scores - top_score)
    return raised / jnp.sum(raised, axis=-1, keepdims=True)


def attend(query, keys, values, query_seg, key_seg, causal, scale):
    count = query.shape[0]
    block = min(512, count)
    query_heads = split_heads(query)
    key_heads = split_heads(keys)
    value_heads = split_heads(values)
    position = jnp.arange(count, dtype=jnp.int32)
    pieces = []
    for start in range(0, count, block):
        stop = start + block
        probs = softmax_block(
            query_heads[start:stop],
            key_heads,
            query_seg[start:stop],
            key_seg,
            position[start:stop],
            position,
            causal,
            scale,
        )
        pieces.append(
            jnp.einsum(
                "hqk,khd->qhd",
                probs.astype(jnp.bfloat16),
                value_heads,
                preferred_element_type=jnp.float32,
            )
        )
    return jnp.concatenate(pieces, axis=0).reshape(count, query.shape[1])


def attend_back(grad_mix, query, keys, values, query_seg, key_seg, causal, scale):
    count = query.shape[0]
    block = min(512, count)
    query_heads = split_heads(query)
    key_heads = split_heads(keys)
    value_heads = split_heads(values)
    grad_heads = split_heads(grad_mix)
    position = jnp.arange(count, dtype=jnp.int32)
    grad_keys = jnp.zeros(key_heads.shape, jnp.float32)
    grad_values = jnp.zeros(value_heads.shape, jnp.float32)
    query_parts = []
    for start in range(0, count, block):
        stop = start + block
        probs = softmax_block(
            query_heads[start:stop],
            key_heads,
            query_seg[start:stop],
            key_seg,
            position[start:stop],
            position,
            causal,
            scale,
        )
        grad_block = grad_heads[start:stop]
        grad_probs = jnp.einsum(
            "qhd,khd->hqk", grad_block, value_heads, preferred_element_type=jnp.float32
        )
        grad_scores = (
            probs * (grad_probs - jnp.sum(probs * grad_probs, axis=-1, keepdims=True))
        ).astype(jnp.bfloat16)
        query_parts.append(
            jnp.einsum("hqk,khd->qhd", grad_scores, key_heads, preferred_element_type=jnp.float32)
            * scale
        )
        grad_keys = (
            grad_keys
            + jnp.einsum(
                "hqk,qhd->khd",
                grad_scores,
                query_heads[start:stop],
                preferred_element_type=jnp.float32,
            )
            * scale
        )
        grad_values = grad_values + jnp.einsum(
            "hqk,qhd->khd",
            probs.astype(jnp.bfloat16),
            grad_block,
            preferred_element_type=jnp.float32,
        )
    grad_query = jnp.concatenate(query_parts, axis=0).reshape(count, -1)
    return (grad_query, grad_keys.reshape(count, -1), grad_values.reshape(count, -1))


def run_layer(rows, params, own_seg, src_seg, is_dec, memory, scale):
    (
        w_query,
        w_key,
        w_value,
        w_out,
        w_up,
        w_down,
        cross_first,
        cross_second,
        norm_gains,
        norm_biases,
        cross_scale,
        cross_shift,
    ) = params
    residual = rows.astype(jnp.float32)
    rows_full = widen(rows)
    query = plain_dot(rows_full, w_query).astype(jnp.bfloat16)
    key_part = plain_dot(rows_full, w_key).astype(jnp.bfloat16)
    value_part = plain_dot(rows_full, w_value).astype(jnp.bfloat16)
    self_mix = attend(query, key_part, value_part, own_seg, own_seg, is_dec, scale).astype(
        jnp.bfloat16
    )
    first_sum = residual + narrow(plain_dot(self_mix, w_out))
    first, first_scaled, first_inverse = norm_rows(first_sum, norm_gains[0], norm_biases[0])
    first_full = widen(first.astype(jnp.bfloat16))
    cross_query = plain_dot(first_full, cross_first).astype(jnp.bfloat16)
    cross_mix = attend(cross_query, memory[0], memory[1], own_seg, src_seg, False, scale).astype(
        jnp.bfloat16
    )
    second_sum = first + narrow(right_dot(cross_mix, cross_second))
    second_norm, second_scaled, second_inverse = norm_rows(second_sum, cross_scale, cross_shift)
    second = jnp.where(is_dec, second_norm, first)
    second_full = widen(second.astype(jnp.bfloat16))
    hidden_pre = plain_dot(second_full, w_up)
    hidden = jax.nn.silu(hidden_pre).astype(jnp.bfloat16)
    third_sum = second + narrow(plain_dot(hidden, w_down))
    result, third_scaled, third_inverse = norm_rows(third_sum, norm_gains[1], norm_biases[1])
    result_full = widen(result.astype(jnp.bfloat16))
    mem_keys = plain_dot(result_full, cross_first).astype(jnp.bfloat16)
    mem_values = plain_dot(result_full, cross_second).astype(jnp.bfloat16)
    return {
        "rows_full": rows_full,
        "query": query,
        "key_part": key_part,
        "value_part": value_part,
        "self_mix": self_mix,
        "first_scaled": first_scaled,
        "first_inverse": first_inverse,
        "first_full": first_full,
        "cross_query": cross_query,
        "cross_mix": cross_mix,
        "memory_keys": memory[0],
        "memory_values": memory[1],
        "second_scaled": second_scaled,
        "second_inverse": second_inverse,
        "second_full": second_full,
        "hidden_pre": hidden_pre,
        "hidden": hidden,
        "third_scaled": third_scaled,
        "third_inverse": third_inverse,
        "result": result,
        "result_full": result_full,
        "mem_keys": mem_keys,
        "mem_values": mem_values,
    }


def layer_back(grad_out, kept, params, own_seg, src_seg, is_dec, scale):
    (
        w_query,
        w_key,
        w_value,
        w_out,
        w_up,
        w_down,
        cross_first,
        cross_second,
        norm_gains,
        norm_biases,
        cross_scale,
        cross_shift,
    ) = params
    grad_third, gain_two, bias_two = norm_back(
        grad_out, kept["third_scaled"], kept["third_inverse"], norm_gains[1]
    )
    grad_down_full = widen(grad_third.astype(jnp.bfloat16))
    grad_w_down = left_dot(kept["hidden"], grad_down_full)
    grad_hidden = right_dot(grad_down_full, w_down)
    silu_pull = jax.vjp(jax.nn.silu, kept["hidden_pre"])[1]
    grad_pre = silu_pull(grad_hidden)[0].astype(jnp.bfloat16)
    grad_w_up = left_dot(kept["second_full"], grad_pre)
    grad_second = grad_third + narrow(right_dot(grad_pre, w_up))
    grad_cross_sum, cross_gain_grad, cross_bias_grad = norm_back(
        grad_second, kept["second_scaled"], kept["second_inverse"], cross_scale
    )
    grad_cross_sum = jnp.where(is_dec, grad_cross_sum, 0.0)
    cross_gain_grad = jnp.where(is_dec, cross_gain_grad, 0.0)
    cross_bias_grad = jnp.where(is_dec, cross_bias_grad, 0.0)
    grad_cross_full = widen(grad_cross_sum.astype(jnp.bfloat16))
    grad_second_weight = left_dot(grad_cross_full, kept["cross_mix"])
    grad_cross_mix = plain_dot(grad_cross_full, cross_second).astype(jnp.bfloat16)
    grad_cross_query, grad_mem_keys, grad_mem_values = attend_back(
        grad_cross_mix,
        kept["cross_query"],
        kept["memory_keys"],
        kept["memory_values"],
        own_seg,
        src_seg,
        False,
        scale,
    )
    grad_cross_query = grad_cross_query.astype(jnp.bfloat16)
    grad_first_weight = left_dot(kept["first_full"], grad_cross_query)
    grad_first = jnp.where(is_dec, grad_cross_sum, grad_second) + narrow(
        right_dot(grad_cross_query, cross_first)
    )
    grad_first_sum, gain_one, bias_one = norm_back(
        grad_first, kept["first_scaled"], kept["first_inverse"], norm_gains[0]
    )
    grad_self_full = widen(grad_first_sum.astype(jnp.bfloat16))
    grad_w_out = left_dot(kept["self_mix"], grad_self_full)
    grad_self_mix = right_dot(grad_self_full, w_out).astype(jnp.bfloat16)
    grad_query, grad_key, grad_value = attend_back(
        grad_self_mix,
        kept["query"],
        kept["key_part"],
        kept["value_part"],
        own_seg,
        own_seg,
        is_dec,
        scale,
    )
    grad_query = grad_query.astype(jnp.bfloat16)
    grad_key = grad_key.astype(jnp.bfloat16)
    grad_value = grad_value.astype(jnp.bfloat16)
    grad_w_query = left_dot(kept["rows_full"], grad_query)
    grad_w_key = left_dot(kept["rows_full"], grad_key)
    grad_w_value = left_dot(kept["rows_full"], grad_value)
    partial_rows = (
        right_dot(grad_query, w_query) + right_dot(grad_key, w_key) + right_dot(grad_value, w_value)
    )
    grad_rows = grad_first_sum + narrow(partial_rows)
    sent_back = (grad_mem_keys.astype(jnp.bfloat16), grad_mem_values.astype(jnp.bfloat16))
    weight_grads = (
        grad_w_query,
        grad_w_key,
        grad_w_value,
        grad_w_out,
        grad_w_up,
        grad_w_down,
        grad_first_weight,
        grad_second_weight,
    )
    norm_grads = (gain_one, gain_two, bias_one, bias_two)
    return (grad_rows, weight_grads, norm_grads, (cross_gain_grad, cross_bias_grad), sent_back)


def body(
    embeddings,
    src_len,
    tgt_len,
    attn_in,
    attn_out,
    ffn_in,
    ffn_out,
    cross_a,
    cross_b,
    norm_gain,
    norm_bias,
    cross_gain,
    cross_bias,
    cotangent,
):
    section_index = lax.axis_index("section")
    is_dec = section_index == 1
    inputs = embeddings[0]
    packs = inputs.shape[0]
    local_rows = inputs.shape[1]
    features = inputs.shape[2]
    total_rows = local_rows * lax.axis_size("mp")
    sentences = src_len.shape[1]
    width = attn_in.shape[3]
    scale = HD ** (-0.5)
    params = (
        attn_in[0, 0],
        attn_in[0, 1],
        attn_in[0, 2],
        attn_out[0],
        ffn_in[0],
        ffn_out[0],
        cross_a[0],
        cross_b[0],
        norm_gain[0],
        norm_bias[0],
        cross_gain,
        cross_bias,
    )
    source_seg = jax.vmap(lambda lengths: segment_ids(lengths, total_rows))(src_len)
    target_seg = jax.vmap(lambda lengths: segment_ids(lengths, total_rows))(tgt_len)
    own_all = jnp.where(is_dec, target_seg, source_seg)
    row_start = lax.axis_index("mp") * local_rows
    live_rows = (
        lax.dynamic_slice_in_dim(target_seg, row_start, local_rows, axis=1) < sentences
    ).astype(jnp.float32)
    blank = jnp.zeros((total_rows, width), jnp.bfloat16)
    received = (blank, blank)
    received_list = []
    layer_rows = jnp.zeros((packs, local_rows, features), jnp.bfloat16)
    for tick_index in range(packs + 1):
        offset = tick_index - section_index
        valid = (offset >= 0) & (offset < packs)
        batch_index = jnp.clip(offset, 0, packs - 1)
        rows = lax.dynamic_index_in_dim(inputs, batch_index, 0, keepdims=False)
        own_seg = lax.dynamic_index_in_dim(own_all, batch_index, 0, keepdims=False)
        src_seg = lax.dynamic_index_in_dim(source_seg, batch_index, 0, keepdims=False)
        kept = run_layer(rows, params, own_seg, src_seg, is_dec, received, scale)
        current = lax.dynamic_index_in_dim(layer_rows, batch_index, 0, keepdims=False)
        layer_rows = lax.dynamic_update_index_in_dim(
            layer_rows,
            jnp.where(valid, kept["result"].astype(jnp.bfloat16), current),
            batch_index,
            0,
        )
        received_list.append(received)
        if tick_index < packs:
            received = passed_along((kept["mem_keys"], kept["mem_values"]), "section", 1)
    received_keys = jnp.stack([entry[0] for entry in received_list])
    received_values = jnp.stack([entry[1] for entry in received_list])
    weight_total = (
        jnp.zeros(params[0].shape, jnp.float32),
        jnp.zeros(params[1].shape, jnp.float32),
        jnp.zeros(params[2].shape, jnp.float32),
        jnp.zeros(params[3].shape, jnp.float32),
        jnp.zeros(params[4].shape, jnp.float32),
        jnp.zeros(params[5].shape, jnp.float32),
        jnp.zeros(params[6].shape, jnp.float32),
        jnp.zeros(params[7].shape, jnp.float32),
    )
    norm_total = tuple((jnp.zeros((features,), jnp.float32) for entry in range(4)))
    cross_total = (jnp.zeros((features,), jnp.float32), jnp.zeros((features,), jnp.float32))
    grad_inputs = jnp.zeros((packs, local_rows, features), jnp.float32)
    returned = (blank, blank)
    for tick_index in range(packs + 1):
        offset = tick_index - 1 + section_index
        valid = (offset >= 0) & (offset < packs)
        batch_index = jnp.clip(offset, 0, packs - 1)
        own_seg = lax.dynamic_index_in_dim(own_all, batch_index, 0, keepdims=False)
        src_seg = lax.dynamic_index_in_dim(source_seg, batch_index, 0, keepdims=False)
        source_tick = batch_index + section_index
        rows = lax.dynamic_index_in_dim(inputs, batch_index, 0, keepdims=False)
        memory = (
            lax.dynamic_index_in_dim(received_keys, source_tick, 0, keepdims=False),
            lax.dynamic_index_in_dim(received_values, source_tick, 0, keepdims=False),
        )
        kept = run_layer(rows, params, own_seg, src_seg, is_dec, memory, scale)
        grad_mem_keys, grad_mem_values = returned
        mem_first = left_dot(kept["result_full"], grad_mem_keys)
        mem_second = left_dot(kept["result_full"], grad_mem_values)
        grad_memory = narrow(
            right_dot(grad_mem_keys, params[6]) + right_dot(grad_mem_values, params[7])
        )
        target_rows = lax.dynamic_index_in_dim(cotangent, batch_index, 0, keepdims=False).astype(
            jnp.float32
        )
        target_rows = (
            target_rows
            * lax.dynamic_index_in_dim(live_rows, batch_index, 0, keepdims=False)[:, None]
        )
        grad_out = jnp.where(is_dec, target_rows, grad_memory) * valid.astype(jnp.float32)
        grad_rows, weight_grads, norm_grads, cross_grads, sent_back = layer_back(
            grad_out, kept, params, own_seg, src_seg, is_dec, scale
        )
        weight_grads = weight_grads[:6] + (
            weight_grads[6] + mem_first,
            weight_grads[7] + mem_second,
        )
        weight_total = tuple(
            (running + addend for running, addend in zip(weight_total, weight_grads))
        )
        norm_total = tuple((running + addend for running, addend in zip(norm_total, norm_grads)))
        cross_total = tuple((running + addend for running, addend in zip(cross_total, cross_grads)))
        current = lax.dynamic_index_in_dim(grad_inputs, batch_index, 0, keepdims=False)
        grad_inputs = lax.dynamic_update_index_in_dim(
            grad_inputs, jnp.where(valid, grad_rows, current), batch_index, 0
        )
        if tick_index < packs:
            returned = passed_along((sent_back[0], sent_back[1]), "section", -1)
    weight_total = jax.tree.map(
        lambda part: part.astype(jnp.float32), lax.psum(shortened(weight_total), "dp")
    )
    norm_total = lax.psum(norm_total, ("dp", "mp"))
    cross_total = lax.psum(cross_total, ("section", "dp", "mp"))
    grad_attn = jnp.stack([weight_total[0], weight_total[1], weight_total[2]])[None]
    grad_gains = jnp.stack([norm_total[0], norm_total[1]])[None]
    grad_biases = jnp.stack([norm_total[2], norm_total[3]])[None]
    return (
        layer_rows[None],
        grad_inputs[None],
        grad_attn,
        weight_total[3][None],
        weight_total[4][None],
        weight_total[5][None],
        weight_total[6][None],
        weight_total[7][None],
        grad_gains,
        grad_biases,
        cross_total[0],
        cross_total[1],
    )


def solution(mesh):
    return jax.shard_map(
        body,
        mesh=mesh,
        in_specs=(
            P("section", "dp", "mp", None),
            P("dp", None),
            P("dp", None),
            P("section", None, None, "mp"),
            P("section", "mp", None),
            P("section", None, "mp"),
            P("section", "mp", None),
            P("section", None, "mp"),
            P("section", None, "mp"),
            P("section", None, None),
            P("section", None, None),
            P(),
            P(),
            P("dp", "mp", None),
        ),
        out_specs=(
            P("section", "dp", "mp", None),
            P("section", "dp", "mp", None),
            P("section", None, None, "mp"),
            P("section", "mp", None),
            P("section", None, "mp"),
            P("section", "mp", None),
            P("section", None, "mp"),
            P("section", None, "mp"),
            P("section", None, None),
            P("section", None, None),
            P(),
            P(),
        ),
        check_vma=False,
    )
```

profile of v0, /device:TPU:0, one launch (start us, length us, event | category | flops | bytes accessed | tf_op | source)
XLA Modules:
  0.0 2098.8 jit_solution(11361348403653766057)
XLA Ops:
  77.7 17.0 reduce-scatter.41.cloned.1.call-done
  144.9 26.9 %reduce-scatter.93.cloned.1.call-done = bf16[256,512]{1,0:T(8,128)(2,1)} async-done(((bf16[1024,512]{1,0:T(8,128)(2,1)}), bf16[256,512]{1,0:T(8,128)(2,1)}) %reduce-scatter.93.cloned.1.call-update) | async-done | bytes 262160 | tf_op jit(solution)/shard_map/reduce_scatter | solution.py:53
  175.3 24.7 %reduce-scatter.43.cloned.1.call-done = bf16[256,512]{1,0:T(8,128)(2,1)} async-done(((bf16[1024,512]{1,0:T(8,128)(2,1)}), bf16[256,512]{1,0:T(8,128)(2,1)}) %reduce-scatter.43.cloned.1.call-update) | async-done | bytes 262160 | tf_op jit(solution)/shard_map/reduce_scatter | solution.py:53
  227.2 24.3 %reduce-scatter.45.cloned.1.call-done = bf16[256,512]{1,0:T(8,128)(2,1)} async-done(((bf16[1024,512]{1,0:T(8,128)(2,1)}), bf16[256,512]{1,0:T(8,128)(2,1)}) %reduce-scatter.45.cloned.1.call-update) | async-done | bytes 262160 | tf_op jit(solution)/shard_map/reduce_scatter | solution.py:53
  338.0 25.6 %reduce-scatter.49.cloned.1.call-done = bf16[256,512]{1,0:T(8,128)(2,1)} async-done(((bf16[1024,512]{1,0:T(8,128)(2,1)}), bf16[256,512]{1,0:T(8,128)(2,1)}) %reduce-scatter.49.cloned.1.call-update) | async-done | bytes 262160 | tf_op jit(solution)/shard_map/reduce_scatter | solution.py:53
  407.6 25.3 %reduce-scatter.51.cloned.1.call-done = bf16[256,512]{1,0:T(8,128)(2,1)} async-done(((bf16[1024,512]{1,0:T(8,128)(2,1)}), bf16[256,512]{1,0:T(8,128)(2,1)}) %reduce-scatter.51.cloned.1.call-update) | async-done | bytes 262160 | tf_op jit(solution)/shard_map/reduce_scatter | solution.py:53
  518.1 27.0 %reduce-scatter.65.cloned.1.call-done = bf16[256,512]{1,0:T(8,128)(2,1)} async-done(((bf16[1024,512]{1,0:T(8,128)(2,1)}), bf16[256,512]{1,0:T(8,128)(2,1)}) %reduce-scatter.65.cloned.1.call-update) | async-done | bytes 262160 | tf_op jit(solution)/shard_map/reduce_scatter | solution.py:53
  548.6 24.4 %reduce-scatter.55.cloned.1.call-done = bf16[256,512]{1,0:T(8,128)(2,1)} async-done(((bf16[1024,512]{1,0:T(8,128)(2,1)}), bf16[256,512]{1,0:T(8,128)(2,1)}) %reduce-scatter.55.cloned.1.call-update) | async-done | bytes 262160 | tf_op jit(solution)/shard_map/reduce_scatter | solution.py:53
  601.7 22.7 %reduce-scatter.57.cloned.1.call-done = bf16[256,512]{1,0:T(8,128)(2,1)} async-done(((bf16[1024,512]{1,0:T(8,128)(2,1)}), bf16[256,512]{1,0:T(8,128)(2,1)}) %reduce-scatter.57.cloned.1.call-update) | async-done | bytes 262160 | tf_op jit(solution)/shard_map/reduce_scatter | solution.py:53
  754.5 19.2 reduce-scatter.67.cloned.1.call-done
  773.6 28.0 %reduce-scatter.95.cloned.1.call-done = bf16[256,512]{1,0:T(8,128)(2,1)} async-done(((bf16[1024,512]{1,0:T(8,128)(2,1)}), bf16[256,512]{1,0:T(8,128)(2,1)}) %reduce-scatter.95.cloned.1.call-update) | async-done | bytes 262160 | tf_op jit(solution)/shard_map/reduce_scatter | solution.py:53
  849.5 27.9 %reduce-scatter.109.cloned.1.call-done = bf16[256,512]{1,0:T(8,128)(2,1)} async-done(((bf16[1024,512]{1,0:T(8,128)(2,1)}), bf16[256,512]{1,0:T(8,128)(2,1)}) %reduce-scatter.109.cloned.1.call-update) | async-done | bytes 262160 | tf_op jit(solution)/shard_map/reduce_scatter | solution.py:53
  880.8 16.8 all-gather.76.cloned.1.call-done
  907.1 21.8 %reduce-scatter.69.cloned.1.call-done = bf16[256,512]{1,0:T(8,128)(2,1)} async-done(((bf16[1024,512]{1,0:T(8,128)(2,1)}), bf16[256,512]{1,0:T(8,128)(2,1)}) %reduce-scatter.69.cloned.1.call-update) | async-done | bytes 262160 | tf_op jit(solution)/shard_map/reduce_scatter | solution.py:53
  931.3 25.6 %reduce-scatter.71.cloned.1.call-done = bf16[256,512]{1,0:T(8,128)(2,1)} async-done(((bf16[1024,512]{1,0:T(8,128)(2,1)}), bf16[256,512]{1,0:T(8,128)(2,1)}) %reduce-scatter.71.cloned.1.call-update) | async-done | bytes 262160 | tf_op jit(solution)/shard_map/reduce_scatter | solution.py:53
  985.2 25.0 %reduce-scatter.73.cloned.1.call-done = bf16[256,512]{1,0:T(8,128)(2,1)} async-done(((bf16[1024,512]{1,0:T(8,128)(2,1)}), bf16[256,512]{1,0:T(8,128)(2,1)}) %reduce-scatter.73.cloned.1.call-update) | async-done | bytes 262160 | tf_op jit(solution)/shard_map/reduce_scatter | solution.py:53
  1047.1 23.9 %reduce-scatter.75.cloned.1.call-done = bf16[256,512]{1,0:T(8,128)(2,1)} async-done(((bf16[1024,512]{1,0:T(8,128)(2,1)}), bf16[256,512]{1,0:T(8,128)(2,1)}) %reduce-scatter.75.cloned.1.call-update) | async-done | bytes 262160 | tf_op jit(solution)/shard_map/reduce_scatter | solution.py:53
  1075.5 16.9 all-gather.86.cloned.1.call-done
  1125.2 26.2 %reduce-scatter.85.cloned.1.call-done = bf16[256,512]{1,0:T(8,128)(2,1)} async-done(((bf16[1024,512]{1,0:T(8,128)(2,1)}), bf16[256,512]{1,0:T(8,128)(2,1)}) %reduce-scatter.85.cloned.1.call-update) | async-done | bytes 262160 | tf_op jit(solution)/shard_map/reduce_scatter | solution.py:53
  1179.3 25.0 %reduce-scatter.87.cloned.1.call-done = bf16[256,512]{1,0:T(8,128)(2,1)} async-done(((bf16[1024,512]{1,0:T(8,128)(2,1)}), bf16[256,512]{1,0:T(8,128)(2,1)}) %reduce-scatter.87.cloned.1.call-update) | async-done | bytes 262160 | tf_op jit(solution)/shard_map/reduce_scatter | solution.py:53
  1296.1 23.1 %reduce-scatter.99.cloned.1.call-done = bf16[256,512]{1,0:T(8,128)(2,1)} async-done(((bf16[1024,512]{1,0:T(8,128)(2,1)}), bf16[256,512]{1,0:T(8,128)(2,1)}) %reduce-scatter.99.cloned.1.call-update) | async-done | bytes 262160 | tf_op jit(solution)/shard_map/reduce_scatter | solution.py:53
  1347.4 22.0 %reduce-scatter.59.cloned.1.call-done = bf16[256,512]{1,0:T(8,128)(2,1)} async-done(((bf16[1024,512]{1,0:T(8,128)(2,1)}), bf16[256,512]{1,0:T(8,128)(2,1)}) %reduce-scatter.59.cloned.1.call-update) | async-done | bytes 262160 | tf_op jit(solution)/shard_map/reduce_scatter | solution.py:53
  1371.7 25.9 %reduce-scatter.101.cloned.1.call-done = bf16[256,512]{1,0:T(8,128)(2,1)} async-done(((bf16[1024,512]{1,0:T(8,128)(2,1)}), bf16[256,512]{1,0:T(8,128)(2,1)}) %reduce-scatter.101.cloned.1.call-update) | async-done | bytes 262160 | tf_op jit(solution)/shard_map/reduce_scatter | solution.py:53
  1489.2 24.8 %reduce-scatter.113.cloned.1.call-done = bf16[256,512]{1,0:T(8,128)(2,1)} async-done(((bf16[1024,512]{1,0:T(8,128)(2,1)}), bf16[256,512]{1,0:T(8,128)(2,1)}) %reduce-scatter.113.cloned.1.call-update) | async-done | bytes 262160 | tf_op jit(solution)/shard_map/reduce_scatter | solution.py:53
  1542.1 21.8 %reduce-scatter.61.cloned.1.call-done = bf16[256,512]{1,0:T(8,128)(2,1)} async-done(((bf16[1024,512]{1,0:T(8,128)(2,1)}), bf16[256,512]{1,0:T(8,128)(2,1)}) %reduce-scatter.61.cloned.1.call-update) | async-done | bytes 262160 | tf_op jit(solution)/shard_map/reduce_scatter | solution.py:53
  1563.9 28.2 %reduce-scatter.115.cloned.1.call-done = bf16[256,512]{1,0:T(8,128)(2,1)} async-done(((bf16[1024,512]{1,0:T(8,128)(2,1)}), bf16[256,512]{1,0:T(8,128)(2,1)}) %reduce-scatter.115.cloned.1.call-update) | async-done | bytes 262160 | tf_op jit(solution)/shard_map/reduce_scatter | solution.py:53
  1645.5 25.0 %reduce-scatter.103.cloned.1.call-done = bf16[256,512]{1,0:T(8,128)(2,1)} async-done(((bf16[1024,512]{1,0:T(8,128)(2,1)}), bf16[256,512]{1,0:T(8,128)(2,1)}) %reduce-scatter.103.cloned.1.call-update) | async-done | bytes 262160 | tf_op jit(solution)/shard_map/reduce_scatter | solution.py:53
  1898.3 22.4 %reduce-scatter.91.cloned.1.call-done = bf16[256,512]{1,0:T(8,128)(2,1)} async-done(((bf16[1024,512]{1,0:T(8,128)(2,1)}), bf16[256,512]{1,0:T(8,128)(2,1)}) %reduce-scatter.91.cloned.1.call-update) | async-done | bytes 262160 | tf_op jit(solution)/shard_map/reduce_scatter | solution.py:53
  1927.5 21.3 %reduce-scatter.105.cloned.1.call-done = bf16[256,512]{1,0:T(8,128)(2,1)} async-done(((bf16[1024,512]{1,0:T(8,128)(2,1)}), bf16[256,512]{1,0:T(8,128)(2,1)}) %reduce-scatter.105.cloned.1.call-update) | async-done | bytes 262160 | tf_op jit(solution)/shard_map/reduce_scatter | solution.py:53
  1954.1 42.6 %all-reduce = (f32[512]{0:T(512)}, f32[512]{0:T(512)}) all-reduce(f32[512]{0:T(512)S(1)} %select_add_fusion.1, f32[512]{0:T(512)S(1)} %select_add_fusion), channel_id=1, replica_groups=mesh['section'=2,'dp'=4,'mp'=4] {'section','dp','mp'}, use_global_device_ids=true, to_apply=%region_228.229 | all-reduce | flops 1024 | bytes 8192 | tf_op jit(solution)/shard_map/psum | solution.py:469
  1996.8 35.1 %all-reduce.1 = (f32[1,512]{1,0:T(1,128)S(1)}, f32[1,512]{1,0:T(1,128)S(1)}, f32[1,512]{1,0:T(1,128)S(1)}, f32[1,512]{1,0:T(1,128)S(1)}) all-reduce(f32[1,512]{1,0:T(1,128)S(1)} %bitcast.1744, f32[1,512]{1,0:T(1,128)S(1)} %bitcast.1746, f32[1,512]{1,0:T(1,128)S(1)} %bitcast.1743, ...), channel_id=1, replica_groups=mesh['section'=2,'dp'=4,'mp'=4] {'dp','mp'}, use_global_device_ids=true, to_apply=%region_213.214 | all-reduce | flops 2048 | bytes 16384 | tf_op jit(solution)/shard_map/psum | solution.py:468
  2062.3 25.2 %reduce-scatter.119.cloned.1.call-done = bf16[256,512]{1,0:T(8,128)(2,1)} async-done(((bf16[1024,512]{1,0:T(8,128)(2,1)}), bf16[256,512]{1,0:T(8,128)(2,1)}) %reduce-scatter.119.cloned.1.call-update) | async-done | bytes 262160 | tf_op jit(solution)/shard_map/reduce_scatter | solution.py:53
  (1735 shorter events, 1285.5 us)
Async XLA Ops:
  12.0 82.8 %reduce-scatter.41.cloned.1.call-start = ((), (), s32[]{:S(2)}) async-start(), calls=%async_computation.40 | async-start | bytes 1310720 | tf_op jit(solution)/shard_map/reduce_scatter | solution.py:53
  122.3 77.7 %reduce-scatter.43.cloned.1.call-start = ((), (), s32[]{:S(2)}) async-start(), calls=%async_computation.42 | async-start | bytes 1310720 | tf_op jit(solution)/shard_map/reduce_scatter | solution.py:53
  137.0 85.6 %all-gather.54.cloned.1.call-start = ((), (), s32[]{:S(2)}) async-start(), calls=%async_computation.43 | async-start | bytes 1310720 | tf_op jit(solution)/shard_map/all_gather | solution.py:49
  288.9 74.6 %reduce-scatter.49.cloned.1.call-start = ((), (), s32[]{:S(2)}) async-start(), calls=%async_computation.48 | async-start | bytes 1310720 | tf_op jit(solution)/shard_map/reduce_scatter | solution.py:53
  390.4 94.7 %all-gather.62.cloned.1.call-start = ((), (), s32[]{:S(2)}) async-start(), calls=%async_computation.52 | async-start | bytes 1310720 | tf_op jit(solution)/shard_map/all_gather | solution.py:49
  468.0 77.1 %reduce-scatter.65.cloned.1.call-start = ((), (), s32[]{:S(2)}) async-start(), calls=%async_computation.63 | async-start | bytes 1310720 | tf_op jit(solution)/shard_map/reduce_scatter | solution.py:53
  485.1 87.9 %reduce-scatter.55.cloned.1.call-start = ((), (), s32[]{:S(2)}) async-start(), calls=%async_computation.54 | async-start | bytes 1310720 | tf_op jit(solution)/shard_map/reduce_scatter | solution.py:53
  516.9 78.6 %all-gather.66.cloned.1.call-start = ((), (), s32[]{:S(2)}) async-start(), calls=%async_computation.55 | async-start | bytes 1310720 | tf_op jit(solution)/shard_map/all_gather | solution.py:49
  600.7 79.1 %all-gather.68.cloned.1.call-start = ((), (), s32[]{:S(2)}) async-start(), calls=%async_computation.58 | async-start | bytes 1310720 | tf_op jit(solution)/shard_map/all_gather | solution.py:49
  657.5 82.5 %reduce-scatter.107.cloned.1.call-start = ((), (), s32[]{:S(2)}) async-start(), calls=%async_computation.99 | async-start | bytes 1310720 | tf_op jit(solution)/shard_map/reduce_scatter | solution.py:53
  664.0 81.6 %all-gather.84.cloned.1.call-start = ((), (), s32[]{:S(2)}) async-start(), calls=%async_computation.76 | async-start | bytes 1310720 | tf_op jit(solution)/shard_map/all_gather | solution.py:49
  667.0 106.7 %reduce-scatter.67.cloned.1.call-start = ((), (), s32[]{:S(2)}) async-start(), calls=%async_computation.65 | async-start | bytes 1310720 | tf_op jit(solution)/shard_map/reduce_scatter | solution.py:53
  725.3 76.4 %reduce-scatter.95.cloned.1.call-start = ((), (), s32[]{:S(2)}) async-start(), calls=%async_computation.89 | async-start | bytes 1310720 | tf_op jit(solution)/shard_map/reduce_scatter | solution.py:53
  739.8 81.6 %all-gather.104.cloned.1.call-start = ((), (), s32[]{:S(2)}) async-start(), calls=%async_computation.100 | async-start | bytes 1310720 | tf_op jit(solution)/shard_map/all_gather | solution.py:49
  1210.4 83.2 %reduce-scatter.97.cloned.1.call-start = ((), (), s32[]{:S(2)}) async-start(), calls=%async_computation.91 | async-start | bytes 1310720 | tf_op jit(solution)/shard_map/reduce_scatter | solution.py:53
  1406.0 80.7 %reduce-scatter.111.cloned.1.call-start = ((), (), s32[]{:S(2)}) async-start(), calls=%async_computation.103 | async-start | bytes 1310720 | tf_op jit(solution)/shard_map/reduce_scatter | solution.py:53
  1612.1 76.8 %all-gather.114.cloned.1.call-start = ((), (), s32[]{:S(2)}) async-start(), calls=%async_computation.111 | async-start | bytes 1310720 | tf_op jit(solution)/shard_map/all_gather | solution.py:49
  1612.8 94.3 %all-gather.82.cloned.1.call-start = ((), (), s32[]{:S(2)}) async-start(), calls=%async_computation.73 | async-start | bytes 1310720 | tf_op jit(solution)/shard_map/all_gather | solution.py:49
  1613.4 121.7 %reduce-scatter.117.cloned.1.call-start = ((), (), s32[]{:S(2)}) async-start(), calls=%async_computation.108 | async-start | bytes 1310720 | tf_op jit(solution)/shard_map/reduce_scatter | solution.py:53
  1626.7 143.2 %all-gather.116.cloned.1.call-start = ((), (), s32[]{:S(2)}) async-start(), calls=%async_computation.112 | async-start | bytes 1310720 | tf_op jit(solution)/shard_map/all_gather | solution.py:49
  1627.3 154.2 %all-gather.118.cloned.1.call-start = ((), (), s32[]{:S(2)}) async-start(), calls=%async_computation.113 | async-start | bytes 1310720 | tf_op jit(solution)/shard_map/all_gather | solution.py:49
  1641.9 147.9 %all-gather.102.cloned.1.call-start = ((), (), s32[]{:S(2)}) async-start(), calls=%async_computation.97 | async-start | bytes 1310720 | tf_op jit(solution)/shard_map/all_gather | solution.py:49
  1675.6 132.7 %all-gather.92.cloned.1.call-start = ((), (), s32[]{:S(2)}) async-start(), calls=%async_computation.85 | async-start | bytes 1310720 | tf_op jit(solution)/shard_map/all_gather | solution.py:49
  1708.9 141.7 %all-gather.120.cloned.1.call-start = ((), (), s32[]{:S(2)}) async-start(), calls=%async_computation.114 | async-start | bytes 1310720 | tf_op jit(solution)/shard_map/all_gather | solution.py:49
  1717.8 137.8 %all-gather.112.cloned.1.call-start = ((), (), s32[]{:S(2)}) async-start(), calls=%async_computation.109 | async-start | bytes 1310720 | tf_op jit(solution)/shard_map/all_gather | solution.py:49
  1739.4 135.7 %all-gather.72.cloned.1.call-start = ((), (), s32[]{:S(2)}) async-start(), calls=%async_computation.61 | async-start | bytes 1310720 | tf_op jit(solution)/shard_map/all_gather | solution.py:49
  1750.7 142.0 %reduce-scatter.77.cloned.1.call-start = ((), (), s32[]{:S(2)}) async-start(), calls=%async_computation.74 | async-start | bytes 1310720 | tf_op jit(solution)/shard_map/reduce_scatter | solution.py:53
  1758.6 162.1 %reduce-scatter.91.cloned.1.call-start = ((), (), s32[]{:S(2)}) async-start(), calls=%async_computation.86 | async-start | bytes 1310720 | tf_op jit(solution)/shard_map/reduce_scatter | solution.py:53
  1828.1 120.8 %reduce-scatter.105.cloned.1.call-start = ((), (), s32[]{:S(2)}) async-start(), calls=%async_computation.98 | async-start | bytes 1310720 | tf_op jit(solution)/shard_map/reduce_scatter | solution.py:53
  1835.3 198.3 %all-reduce.5.cloned.1.call-start = ((), (), s32[]{:S(2)}) async-start(), calls=%async_computation.123 | async-start | bytes 3670016 | tf_op jit(solution)/shard_map/psum | solution.py:466
  1874.1 185.9 %reduce-scatter.63.cloned.1.call-start = ((), (), s32[]{:S(2)}) async-start(), calls=%async_computation.62 | async-start | bytes 1310720 | tf_op jit(solution)/shard_map/reduce_scatter | solution.py:53
  1879.0 208.5 %reduce-scatter.119.cloned.1.call-start = ((), (), s32[]{:S(2)}) async-start(), calls=%async_computation.110 | async-start | bytes 1310720 | tf_op jit(solution)/shard_map/reduce_scatter | solution.py:53
  (543 other events, 11222.4 us)
Sparse Core Ops, SparseCore 0:
  69.7 24.9 reduce-scatter.40
  118.8 24.8 reduce-scatter.46
  146.9 24.8 reduce-scatter.92
  175.1 24.8 reduce-scatter.42
  226.5 24.8 reduce-scatter.44
  310.8 24.8 reduce-scatter.52
  338.6 24.8 reduce-scatter.48
  408.0 24.8 reduce-scatter.50
  492.0 24.8 reduce-scatter.78
  520.2 24.8 reduce-scatter.64
  548.1 24.8 reduce-scatter.54
  599.5 24.8 reduce-scatter.56
  701.6 24.9 reduce-scatter.106
  748.7 24.9 reduce-scatter.66
  776.8 24.8 reduce-scatter.94
  824.5 24.8 reduce-scatter.80
  904.0 24.8 reduce-scatter.68
  985.2 24.8 reduce-scatter.72
  1179.3 24.8 reduce-scatter.86
  1266.0 24.8 reduce-scatter.96
  1294.2 24.8 reduce-scatter.98
  1344.4 24.9 reduce-scatter.58
  1460.8 24.8 reduce-scatter.110
  1489.0 24.9 reduce-scatter.112
  1539.0 24.9 reduce-scatter.60
  1567.2 24.8 reduce-scatter.114
  1617.5 24.8 reduce-scatter.88
  1867.7 24.8 reduce-scatter.76
  1895.8 24.8 reduce-scatter.90
  1923.9 24.8 reduce-scatter.104
  1951.7 81.8 all-reduce.4
  2062.6 24.8 reduce-scatter.118
  (52 shorter events, 941.8 us)
where the time goes:
time: 2110 us; the launch traced here: 2100 us
  waiting for transfers between devices  1130 us (54%)
  matrix products  547 us (26%)
  other arithmetic  201 us (10%)
  local copies, waits for them, and re-layouts  89.5 us (4%)
  blocking collectives  77.6 us (4%)
  starting transfers between devices  29.9 us (1%)
  between operations  21.8 us (1%)
    reduce_scatter x40, waiting for transfers between devices, narrow(): lax.psum_scatter(partial_value.astype(jnp.bfloat16), 'mp', scatter_dimens...  750 us
    all_gather x43, waiting for transfers between devices, widen(): return lax.all_gather(rows, 'mp', axis=0, tiled=True)  340 us
    sub x32, matrix products, softmax_block(): raised = jnp.exp(scores - top_score)  148 us
    dot_general x62, matrix products, plain_dot(): return jnp.dot(left, right, preferred_element_type=jnp.float32)  109 us
    dot_general x32, matrix products, attend(): jnp.einsum('hqk,khd->qhd', probs.astype(jnp.bfloat16), value_heads, prefe...  66.5 us
    dot_general x44, matrix products, right_dot(): lax.dot_general(left, right, (((1,), (1,)), ((), ())), preferred_element_...  64.7 us
    dot_general x39, matrix products, left_dot(): lax.dot_general(left, right, (((0,), (0,)), ((), ())), preferred_element_...  62 us
    unnamed x960, local copies, waits for them, and re-layouts  55.7 us
  transfers between devices with their start and end apart: 96, of which 73 were waited for; matrix products, arithmetic and copies ran while one was open for 32% of the time, Pallas kernels for 0%

commit v1 on v0

v1 whole, which is shorter than its diff:
```python
import functools

import jax
import jax.numpy as jnp
from jax import lax
from jax.experimental import pallas as pl
from jax.experimental.pallas import tpu as pltpu
from jax.sharding import PartitionSpec as P

HD = 64
EPS = 1e-05
NEG = -1000000000.0
F32 = jnp.float32
BF16 = jnp.bfloat16
QC = 256


def nn(left, right):
    return lax.dot_general(left, right, (((1,), (0,)), ((), ())), preferred_element_type=F32)


def nt(left, right):
    return lax.dot_general(left, right, (((1,), (1,)), ((), ())), preferred_element_type=F32)


def tn(left, right):
    return lax.dot_general(left, right, (((0,), (0,)), ((), ())), preferred_element_type=F32)


def hop(value, distance):
    count = lax.axis_size("mp")
    return lax.ppermute(value, "mp", [(i, i ^ distance) for i in range(count)])


def gather(own):
    far = hop(own, 2)
    return own, hop(own, 1), far, hop(far, 1)


def exchange(blocks):
    return [blocks[0]] + [hop(blocks[r], r) for r in range(1, 4)]


def reduce_rows(even, odd):
    near = hop(odd, 1)
    far = hop((even[1].astype(F32) + near[1].astype(F32)).astype(BF16), 2)
    return even[0].astype(F32) + near[0].astype(F32) + far.astype(F32)


def section_send(value, source):
    return lax.ppermute(value, "section", [(source, 1 - source)])


def chain_sum(values):
    count = lax.axis_size("dp")
    if count == 1:
        return values
    if count % 2:
        return lax.psum(values, "dp")
    index = lax.axis_index("dp")
    for i in range(count // 2 - 1):
        moved = lax.ppermute(values, "dp", [(i, i + 1), (count - 1 - i, count - 2 - i)])
        values = (values.astype(F32) + moved.astype(F32)).astype(BF16)
    middle = count // 2
    moved = lax.ppermute(values, "dp", [(middle - 1, middle), (middle, middle - 1)])
    values = (values.astype(F32) + moved.astype(F32)).astype(BF16)
    for i in reversed(range(count // 2 - 1)):
        moved = lax.ppermute(values, "dp", [(i + 1, i), (count - 2 - i, count - 1 - i)])
        values = jnp.where((index == i) | (index == count - 1 - i), moved, values)
    return values


def tree_sum(value):
    value = value + hop(value, 1)
    value = value + hop(value, 2)
    count = lax.axis_size("dp")
    if count & (count - 1):
        return lax.psum(value, "dp")
    step = 1
    while step < count:
        value = value + lax.ppermute(value, "dp", [(i, i ^ step) for i in range(count)])
        step *= 2
    return value


def pack_layout(lengths, pack, sentences):
    ends, start, largest, top, end = [], 0, 0, 0, 0
    for j in range(sentences):
        size = lengths[pack, j]
        better = size > top
        start = jnp.where(better, end, start)
        largest = jnp.where(better, j, largest)
        top = jnp.where(better, size, top)
        end = end + size
        ends.append(end)
    return ends, start, largest


def segment_ids(ends, shift, first, shape, dim, total):
    at = lax.broadcasted_iota(jnp.int32, shape, dim) + (first + shift)
    at = jnp.where(at >= total, at - total, at)
    return sum(jnp.where(at >= end, 1, 0) for end in ends)


def center_rows(total):
    center = jnp.mean(total, axis=-1, keepdims=True)
    centred = total - center
    inverse = lax.rsqrt(jnp.mean(centred * centred, axis=-1, keepdims=True) + EPS)
    return centred * inverse, inverse


def norm_back(grad, scaled, inverse, gain):
    inner = grad * gain
    first = jnp.mean(inner, axis=-1, keepdims=True)
    second = jnp.mean(inner * scaled, axis=-1, keepdims=True)
    return (
        inverse * (inner - first - scaled * second),
        jnp.sum(grad * scaled, axis=0, keepdims=True),
        jnp.sum(grad, axis=0, keepdims=True),
    )


def place(roll, slot, me, block, rows, value):
    count = roll.shape[1] // 2
    start = pl.multiple_of((me ^ block) * rows, rows)
    roll[slot, pl.ds(start, rows), :] = value
    roll[slot, pl.ds(start + count, rows), :] = value


def rolled(roll, slot, shift, half, size):
    return roll[slot, pl.ds(shift + half * size, size), :]


def unroll_into(roll, slot, shift, source, half):
    roll[slot, pl.ds(shift + half, half), :] = source[0:half, :]
    roll[slot, pl.ds(shift + 2 * half, half), :] = source[half : 2 * half, :]
    roll[slot, pl.ds(shift, half), :] = source[half : 2 * half, :]


def unrolled(roll, slot, me, block, rows, half):
    return roll[slot, pl.ds(pl.multiple_of(half + (me ^ block) * rows, rows), rows), :]


def head_masks(width):
    lane = lax.broadcasted_iota(jnp.int32, (1, width), 1)
    return [
        jnp.where((lane >= h * HD) & (lane < (h + 1) * HD), 1.0, 0.0).astype(BF16)
        for h in range(width // HD)
    ]


def attend_chunk(keys, values, query, bias, masks):
    tops, sums, outs = [], [], []
    for h, mask in enumerate(masks):
        scores = nt(keys, query * mask) + bias
        top = jnp.max(scores, axis=0, keepdims=True)
        raised = jnp.exp(scores - top)
        total = jnp.sum(raised, axis=0, keepdims=True)
        mixed = tn(values, raised.astype(BF16))
        outs.append(mixed[h * HD : (h + 1) * HD, :] / total)
        sums.append(top + jnp.log(total))
    return jnp.concatenate(outs, axis=0).T, sums


def attend_back_chunk(keys, values, query, grad, out, lse, bias, masks):
    folded = (grad.astype(F32) * out).T
    grad_query = []
    probs, grads = [], []
    for h, mask in enumerate(masks):
        scores = nt(keys, query * mask) + bias
        prob = jnp.exp(scores - lse[h])
        grad_prob = nt(values, grad * mask)
        inner = jnp.sum(folded[h * HD : (h + 1) * HD, :], axis=0, keepdims=True)
        grad_score = (prob * (grad_prob - inner)).astype(BF16)
        probs.append(prob.astype(BF16))
        grads.append(grad_score)
        grad_query.append(tn(keys, grad_score)[h * HD : (h + 1) * HD, :])
    grad_keys = sum(nn(g, query * m) for g, m in zip(grads, masks))
    grad_values = sum(nn(p, grad * m) for p, m in zip(probs, masks))
    return jnp.concatenate(grad_query, axis=0).T * (HD ** (-0.5)), grad_keys, grad_values


def self_bias(is_dec, ends, shift, bias, half):
    key = lax.broadcasted_iota(jnp.int32, (half, QC), 0)
    key_ids = segment_ids(ends, shift, half, (half, 1), 0, 2 * half)
    for c in range(half // QC):
        cols = slice(c * QC, (c + 1) * QC)
        query = lax.broadcasted_iota(jnp.int32, (half, QC), 1) + c * QC
        query_ids = segment_ids(ends, shift, half + c * QC, (1, QC), 1, 2 * half)
        allowed = (key <= query) | (is_dec == 0)
        bias[0, :, cols] = jnp.where(allowed, 0.0, NEG)
        bias[1, :, cols] = jnp.where(allowed & (key_ids == query_ids), 0.0, NEG)


def cross_bias(source, target, own_keys, bias, half):
    for kind in range(2):
        query_ids = segment_ids(target[0], target[1], kind * half, (1, half), 1, 2 * half)
        for part in range(kind + 1):
            first = part * half if kind else own_keys
            key_ids = segment_ids(source[0], source[1], first, (half, 1), 0, 2 * half)
            rows = slice(part * half, (part + 1) * half)
            bias[kind, rows, :] = jnp.where(key_ids == query_ids, 0.0, NEG)


def place_of():
    return lax.axis_index("section"), lax.axis_index("mp")


def own_layout(source, target, is_dec, pack):
    sentences = source.shape[1]
    first, second = pack_layout(source, pack, sentences), pack_layout(target, pack, sentences)
    return [jnp.where(is_dec == 1, b, a) for a, b in zip(first[0], second[0])], jnp.where(
        is_dec == 1, second[1], first[1]
    )


def self_forward(
    pack, source, target, x0, x1, x2, x3, weights,
    o0, o1, o2, o3, query, keys, values, lse, outs, roll, bias,
):
    is_dec, me = place_of()
    ends, shift = own_layout(source, target, is_dec, pack)
    rows = x0.shape[1]
    half = 2 * rows
    for block, x in enumerate((x0, x1, x2, x3)):
        for slot in range(3):
            value = nn(x[pack], weights[slot])
            if slot == 0:
                value = value.astype(BF16).astype(F32) * (HD ** (-0.5))
            place(roll, slot, me, block, rows, value)
    for h in range(2):
        part = slice(h * half, (h + 1) * half)
        query[part, :] = rolled(roll, 0, shift, h, half).astype(BF16)
        keys[part, :] = rolled(roll, 1, shift, h, half).astype(BF16)
        values[part, :] = rolled(roll, 2, shift, h, half).astype(BF16)
    self_bias(is_dec, ends, shift, bias, half)
    masks = head_masks(query.shape[1])
    chunks = half // QC

    def step(i, carry):
        h, c = i // chunks, i % chunks
        at = pl.multiple_of(i * QC, QC)
        part = pl.ds(pl.multiple_of(h * half, half), half)
        out, sums = attend_chunk(
            keys[part, :],
            values[part, :],
            query[pl.ds(at, QC), :],
            bias[h, :, pl.ds(pl.multiple_of(c * QC, QC), QC)],
            masks,
        )
        outs[pl.ds(at, QC), :] = out
        for k, row in enumerate(sums):
            lse[k : k + 1, pl.ds(at, QC)] = row
        return carry

    lax.fori_loop(0, 2 * chunks, step, 0)
    unroll_into(roll, 0, shift, outs, half)
    for block, o in enumerate((o0, o1, o2, o3)):
        o[...] = unrolled(roll, 0, me, block, rows, half).astype(BF16)


def self_backward(
    pack, source, target, g0, g1, g2, g3, query, keys, values, lse, outs, x0, x1, x2, x3, weights, *rest,
):
    total = rest[0] if pack else None
    even, odd, new_total, roll, bias, grads, grad_out = rest[1:] if pack else rest
    is_dec, me = place_of()
    ends, shift = own_layout(source, target, is_dec, pack)
    rows = x0.shape[1]
    half = 2 * rows
    for block, g in enumerate((g0, g1, g2, g3)):
        place(roll, 0, me, block, rows, g[...].astype(F32))
    for h in range(2):
        grad_out[h * half : (h + 1) * half, :] = rolled(roll, 0, shift, h, half).astype(BF16)
    self_bias(is_dec, ends, shift, bias, half)
    masks = head_masks(query.shape[1])
    chunks = half // QC
    grads[1] = jnp.zeros(grads.shape[1:], F32)
    grads[2] = jnp.zeros(grads.shape[1:], F32)

    def step(i, carry):
        h, c = i // chunks, i % chunks
        at = pl.ds(pl.multiple_of(i * QC, QC), QC)
        part = pl.ds(pl.multiple_of(h * half, half), half)
        dq, dk, dv = attend_back_chunk(
            keys[part, :],
            values[part, :],
            query[at, :],
            grad_out[at, :],
            outs[at, :],
            [lse[k : k + 1, at] for k in range(len(masks))],
            bias[h, :, pl.ds(pl.multiple_of(c * QC, QC), QC)],
            masks,
        )
        grads[0, at, :] = dq
        grads[1, part, :] += dk
        grads[2, part, :] += dv
        return carry

    lax.fori_loop(0, 2 * chunks, step, 0)
    for slot in range(3):
        unroll_into(roll, slot, shift, grads.at[slot], half)
    for block, x in enumerate((x0, x1, x2, x3)):
        parts = [
            unrolled(roll, slot, me, block, rows, half).astype(BF16) for slot in range(3)
        ]
        sums = odd if block & 1 else even
        sums[block >> 1] = sum(nt(parts[slot], weights[slot]) for slot in range(3)).astype(BF16)
        for slot in range(3):
            grad = tn(x[pack], parts[slot])
            base = total if block == 0 else new_total
            new_total[slot] = grad if base is None else base[slot] + grad


def cross_forward(
    pack, source, target, q0, q1, q2, q3, e0, e1, e2, e3, weights,
    o0, o1, o2, o3, query, keys, values, lse, outs, roll, bias,
):
    is_dec, me = place_of()

    @pl.when(is_dec == 1)
    def _():
        sentences = source.shape[1]
        source_ends, source_shift, source_big = pack_layout(source, pack, sentences)
        ends, shift, big = pack_layout(target, pack, sentences)
        rows = q0.shape[0]
        half = 2 * rows
        own_keys = pl.multiple_of(jnp.where(source_big == big, 0, half), half)
        for block, (q, e) in enumerate(zip((q0, q1, q2, q3), (e0, e1, e2, e3))):
            place(roll, 0, me, block, rows, q[...].astype(F32) * (HD ** (-0.5)))
            place(roll, 1, me, block, rows, nn(e[...], weights[0]))
            place(roll, 2, me, block, rows, nn(e[...], weights[1]))
        for h in range(2):
            part = slice(h * half, (h + 1) * half)
            query[part, :] = rolled(roll, 0, shift, h, half).astype(BF16)
            keys[part, :] = rolled(roll, 1, source_shift, h, half).astype(BF16)
            values[part, :] = rolled(roll, 2, source_shift, h, half).astype(BF16)
        cross_bias((source_ends, source_shift), (ends, shift), own_keys, bias, half)
        masks = head_masks(query.shape[1])

        def run(i, kind, key_rows):
            at = pl.multiple_of(kind * half + i * QC, QC)
            out, sums = attend_chunk(
                keys[key_rows, :],
                values[key_rows, :],
                query[pl.ds(at, QC), :],
                bias[kind, 0 : key_rows.size, pl.ds(pl.multiple_of(i * QC, QC), QC)],
                masks,
            )
            outs[pl.ds(at, QC), :] = out
            for k, row in enumerate(sums):
                lse[k : k + 1, pl.ds(at, QC)] = row

        def step(i, carry):
            run(i, 0, pl.ds(own_keys, half))
            run(i, 1, pl.ds(0, 2 * half))
            return carry

        lax.fori_loop(0, half // QC, step, 0)
        unroll_into(roll, 0, shift, outs, half)
        for block, o in enumerate((o0, o1, o2, o3)):
            o[...] = unrolled(roll, 0, me, block, rows, half).astype(BF16)


def cross_backward(
    pack, source, target, g0, g1, g2, g3, query, keys, values, lse, outs, e0, e1, e2, e3, weights, *rest,
):
    total = rest[0] if pack else None
    c0, c1, c2, c3, even, odd, new_total, roll, bias, grads, grad_out = rest[1:] if pack else rest
    is_dec, me = place_of()

    @pl.when(is_dec == 1)
    def _():
        sentences = source.shape[1]
        source_ends, source_shift, source_big = pack_layout(source, pack, sentences)
        ends, shift, big = pack_layout(target, pack, sentences)
        rows = g0.shape[0]
        half = 2 * rows
        own_keys = pl.multiple_of(jnp.where(source_big == big, 0, half), half)
        for block, g in enumerate((g0, g1, g2, g3)):
            place(roll, 0, me, block, rows, g[...].astype(F32))
        for h in range(2):
            grad_out[h * half : (h + 1) * half, :] = rolled(roll, 0, shift, h, half).astype(BF16)
        cross_bias((source_ends, source_shift), (ends, shift), own_keys, bias, half)
        masks = head_masks(query.shape[1])
        grads[1] = jnp.zeros(grads.shape[1:], F32)
        grads[2] = jnp.zeros(grads.shape[1:], F32)

        def run(i, kind, key_rows):
            at = pl.ds(pl.multiple_of(kind * half + i * QC, QC), QC)
            dq, dk, dv = attend_back_chunk(
                keys[key_rows, :],
                values[key_rows, :],
                query[at, :],
                grad_out[at, :],
                outs[at, :],
                [lse[k : k + 1, at] for k in range(len(masks))],
                bias[kind, 0 : key_rows.size, pl.ds(pl.multiple_of(i * QC, QC), QC)],
                masks,
            )
            grads[0, at, :] = dq
            grads[1, key_rows, :] += dk
            grads[2, key_rows, :] += dv

        def step(i, carry):
            run(i, 0, pl.ds(own_keys, half))
            run(i, 1, pl.ds(0, 2 * half))
            return carry

        lax.fori_loop(0, half // QC, step, 0)
        unroll_into(roll, 0, shift, grads.at[0], half)
        unroll_into(roll, 1, source_shift, grads.at[1], half)
        unroll_into(roll, 2, source_shift, grads.at[2], half)
        for block, (c, e) in enumerate(zip((c0, c1, c2, c3), (e0, e1, e2, e3))):
            parts = [
                unrolled(roll, slot, me, block, rows, half).astype(BF16) for slot in range(3)
            ]
            c[...] = parts[0]
            sums = odd if block & 1 else even
            sums[block >> 1] = (nt(parts[1], weights[0]) + nt(parts[2], weights[1])).astype(BF16)
            for slot in range(2):
                grad = tn(e[...], parts[slot + 1])
                base = total if block == 0 else new_total
                new_total[slot] = grad if base is None else base[slot] + grad


def silu_parts(hidden):
    gate = 1.0 / (1.0 + jnp.exp(-hidden))
    return hidden * gate, gate


def split_weights(stacked):
    width = stacked.shape[0] - 2 * stacked.shape[1]
    inner = (stacked.shape[0] - width) // 2
    return pl.ds(0, width), pl.ds(width, inner), pl.ds(width + inner, inner)


def ffn_forward(normed, shares, out):
    _, up, down = split_weights(shares[0])
    for k, share in enumerate(shares):
        hidden = nn(normed, share[up, :])
        part = nn(silu_parts(hidden)[0].astype(BF16), share[down, :])
        out[...] = part if k == 0 else out[...] + part


def ffn_backward(normed, grad, shares, kept, grad_kept, out):
    _, up, down = split_weights(shares[0])
    for k, share in enumerate(shares):
        hidden = nn(normed, share[up, :])
        value, gate = silu_parts(hidden)
        kept[k] = value.astype(BF16)
        slope = gate * (1.0 + hidden * (1.0 - gate))
        grad_pre = (nt(grad, share[down, :]) * slope).astype(BF16)
        grad_kept[k] = grad_pre
        part = nt(grad_pre, share[up, :])
        out[...] = part if k == 0 else out[...] + part


def after_self(
    pack, m0, m1, m2, m3, x, w0, w1, w2, w3, k0, k1, k2, k3, gains, biases,
    scaled, inverse, low, encoded, scaled_two, inverse_two, c0, c1, c2, c3, work,
):
    is_dec, _ = place_of()
    shares = (w0, w1, w2, w3)
    rows = split_weights(w0)[0]
    total = x[pack].astype(F32)
    for mixed, share in zip((m0, m1, m2, m3), shares):
        total = total + nn(mixed[...], share[rows, :])
    first_scaled, first_inverse = center_rows(total)
    scaled[...] = first_scaled
    inverse[...] = first_inverse
    first = first_scaled * gains[0:1, :] + biases[0:1, :]
    low[...] = first.astype(BF16)

    @pl.when(is_dec == 1)
    def _():
        for c, share in zip((c0, c1, c2, c3), (k0, k1, k2, k3)):
            c[...] = nn(low[...], share[0]).astype(BF16)

    @pl.when(is_dec == 0)
    def _():
        ffn_forward(low[...], shares, work)
        again = scaled[...] * gains[0:1, :] + biases[0:1, :]
        second_scaled, second_inverse = center_rows(again + work[...])
        scaled_two[...] = second_scaled
        inverse_two[...] = second_inverse
        encoded[...] = (second_scaled * gains[1:2, :] + biases[1:2, :]).astype(BF16)


def after_cross(
    pack, target, m0, m1, m2, m3, scaled, w0, w1, w2, w3, k0, k1, k2, k3,
    gains, biases, cross_gain, cross_shift, cotangent,
    decoded, low, grad_low, hidden, grad_hidden, out_low, g0, g1, g2, g3, grad_two, norms, work, kept,
):
    is_dec, me = place_of()

    @pl.when(is_dec == 1)
    def _():
        shares = (w0, w1, w2, w3)
        rows = scaled.shape[0]
        total = scaled[...] * gains[0:1, :] + biases[0:1, :]
        for mixed, share in zip((m0, m1, m2, m3), (k0, k1, k2, k3)):
            total = total + nt(mixed[...], share[1])
        second_scaled, second_inverse = center_rows(total)
        kept[...] = second_scaled
        low[...] = (second_scaled * cross_gain[...] + cross_shift[...]).astype(BF16)
        ffn_forward(low[...], shares, work)
        second = kept[...] * cross_gain[...] + cross_shift[...]
        third_scaled, third_inverse = center_rows(second + work[...])
        decoded[...] = (third_scaled * gains[1:2, :] + biases[1:2, :]).astype(BF16)
        at = lax.broadcasted_iota(jnp.int32, (rows, 1), 0) + me * rows
        end = pack_layout(target, pack, target.shape[1])[0][-1]
        grad = jnp.where(at < end, cotangent[pack].astype(F32), 0.0)
        grad_third, gain_two, bias_two = norm_back(grad, third_scaled, third_inverse, gains[1:2, :])
        grad_low[...] = grad_third.astype(BF16)
        grad_two[...] = grad_third
        ffn_backward(low[...], grad_low[...], shares, hidden, grad_hidden, work)
        grad_second, cross_gain_grad, cross_bias_grad = norm_back(
            grad_two[...] + work[...], kept[...], second_inverse, cross_gain[...]
        )
        grad_two[...] = grad_second
        out_low[...] = grad_second.astype(BF16)
        for g, share in zip((g0, g1, g2, g3), (k0, k1, k2, k3)):
            g[...] = nn(out_low[...], share[1]).astype(BF16)
        norms[...] = jnp.zeros(norms.shape, F32)
        norms[1:2, :] = gain_two
        norms[3:4, :] = bias_two
        norms[4:5, :] = cross_gain_grad
        norms[5:6, :] = cross_bias_grad


def before_self(
    pack, scaled, inverse, low, gains, w0, w1, w2, w3, k0, k1, k2, k3, grad_encoded, scaled_two, inverse_two,
    c0, c1, c2, c3, grad_two, norms_in,
    grad_rows, out_low, g0, g1, g2, g3, grad_low, hidden, grad_hidden, norms, work,
):
    is_dec, _ = place_of()
    shares = (w0, w1, w2, w3)
    rows = split_weights(w0)[0]

    @pl.when(is_dec == 0)
    def _():
        grad_sum, gain_two, bias_two = norm_back(
            grad_encoded[...].astype(F32), scaled_two[...], inverse_two[...], gains[1:2, :]
        )
        grad_low[...] = grad_sum.astype(BF16)
        grad_rows[...] = grad_sum
        ffn_backward(low[...], grad_low[...], shares, hidden, grad_hidden, work)
        work[...] += grad_rows[...]
        norms[...] = jnp.zeros(norms.shape, F32)
        norms[1:2, :] = gain_two
        norms[3:4, :] = bias_two

    @pl.when(is_dec == 1)
    def _():
        total = grad_two[...]
        for grad, share in zip((c0, c1, c2, c3), (k0, k1, k2, k3)):
            total = total + nt(grad[...], share[0])
        work[...] = total
        norms[...] = norms_in[...]

    grad_first, gain_one, bias_one = norm_back(work[...], scaled[...], inverse[...], gains[0:1, :])
    norms[0:1, :] = gain_one
    norms[2:3, :] = bias_one
    grad_rows[...] = grad_first
    out_low[...] = grad_first.astype(BF16)
    for g, share in zip((g0, g1, g2, g3), shares):
        g[...] = nt(out_low[...], share[rows, :]).astype(BF16)


def ffn_grads(packs, *refs):
    is_dec, _ = place_of()
    groups = [refs[i * packs : (i + 1) * packs] for i in range(8)]
    up_even, up_odd, down_even, down_odd = refs[8 * packs :]

    def run(inputs, hiddens, grads, grad_hiddens):
        for k in range(4):
            up, down = (up_odd, down_odd) if k & 1 else (up_even, down_even)
            down[k >> 1] = sum(tn(h[k], g[...]) for h, g in zip(hiddens, grads)).astype(BF16)
            up[k >> 1] = sum(tn(x[...], h[k]) for x, h in zip(inputs, grad_hiddens)).astype(BF16)

    @pl.when(is_dec == 1)
    def _():
        run(*groups[:4])

    @pl.when(is_dec == 0)
    def _():
        run(*groups[4:])


def projection_grads(packs, *refs):
    is_dec, _ = place_of()
    take = lambda n, at: [refs[at + i * n : at + (i + 1) * n] for i in range(packs)]
    mixes, outs = take(4, 0), refs[4 * packs : 5 * packs]
    queries, lows = take(4, 5 * packs), refs[9 * packs : 10 * packs]
    crosses, cross_outs = take(4, 10 * packs), refs[14 * packs : 15 * packs]
    out_even, out_odd, cross_even, cross_odd = refs[15 * packs :]
    for k in range(4):
        target = out_odd if k & 1 else out_even
        target[k >> 1] = sum(tn(m[k][...], g[...]) for m, g in zip(mixes, outs)).astype(BF16)

    @pl.when(is_dec == 1)
    def _():
        for k in range(4):
            target = cross_odd if k & 1 else cross_even
            target[k >> 1, 0] = sum(tn(x[...], q[k][...]) for x, q in zip(lows, queries)).astype(BF16)
            target[k >> 1, 1] = sum(tn(g[...], c[k][...]) for g, c in zip(cross_outs, crosses)).astype(BF16)


def call(kernel, scalars, outs, scratch, micros, *operands):
    space = pl.BlockSpec(memory_space=pltpu.VMEM)
    operands = [pltpu.with_memory_space_constraint(x, pltpu.VMEM) for x in operands]
    return pl.pallas_call(
        kernel,
        out_shape=[pltpu.VMEM(shape, kind) for shape, kind in outs],
        in_specs=[pl.BlockSpec(memory_space=pltpu.SMEM)] * len(scalars) + [space] * len(operands),
        out_specs=[space] * len(outs),
        scratch_shapes=[pltpu.VMEM(shape, kind) for shape, kind in scratch],
        compiler_params=pltpu.CompilerParams(vmem_limit_bytes=24 * 1024 * 1024),
        cost_estimate=pl.CostEstimate(
            flops=int(micros * 1e9), bytes_accessed=1 << 16, transcendentals=0
        ),
    )(*scalars, *operands)


def body(
    embeddings, src_len, tgt_len, attn_in, attn_out, ffn_in, ffn_out, cross_a, cross_b,
    norm_gain, norm_bias, cross_gain, cross_bias_vec, cotangent,
):
    is_dec = lax.axis_index("section") == 1
    x_all = embeddings[0]
    packs, rows, features = x_all.shape
    total_rows = rows * lax.axis_size("mp")
    half = total_rows // 2
    width = attn_in.shape[3]
    hidden = ffn_in.shape[2]
    share_rows = width + 2 * hidden
    gains, biases = norm_gain[0], norm_bias[0]
    cgain, cbias = cross_gain[None, :], cross_bias_vec[None, :]
    lens = (src_len, tgt_len)
    every = range(packs)

    xs = gather(x_all)
    w_self = attn_in[0]
    share = jnp.concatenate([attn_out[0], ffn_in[0], ffn_out[0]], axis=0)
    cross_share = jnp.stack([cross_a[0], cross_b[0]])
    xs, share, cross_share = lax.optimization_barrier((xs, share, cross_share))
    shares = gather(share)
    cross_shares = gather(cross_share)
    memory_weights = section_send(cross_share, 0)

    blocks = [((rows, width), BF16)] * 4
    saved_spec = [((total_rows, width), BF16)] * 3 + [((8, total_rows), F32), ((total_rows, width), F32)]
    roll_spec = ((3, 2 * total_rows, width), F32)
    back_spec = [((3, total_rows, width), F32), ((total_rows, width), BF16)]
    full = (rows, features)
    column = ((rows, 1), F32)
    hid_spec = ((4, rows, hidden), BF16)
    self_scratch = [roll_spec, ((2, half, half), F32)]
    cross_scratch = [roll_spec, ((2, total_rows, half), F32)]
    part = functools.partial

    saved, mixes = [], []
    for p in every:
        out = call(
            part(self_forward, p), lens, blocks + saved_spec, self_scratch, 5.0, *xs, w_self,
        )
        mixes.append(exchange(out[:4]))
        saved.append(out[4:])

    firsts, queries, memories = [], [], []
    for p in every:
        out = call(
            part(after_self, p), (),
            [(full, F32), column, (full, BF16), (full, BF16), (full, F32), column] + blocks,
            [(full, F32)], 4.0,
            *mixes[p], x_all, *shares, *cross_shares, gains, biases,
        )
        firsts.append(out[:6])
        queries.append(exchange(out[6:]))
        memories.append(gather(section_send(out[3], 0)))

    cross_saved, cross_mixes = [], []
    for p in every:
        out = call(
            part(cross_forward, p), lens, blocks + saved_spec, cross_scratch, 6.0,
            *queries[p], *memories[p], memory_weights,
        )
        cross_mixes.append(exchange(out[:4]))
        cross_saved.append(out[4:])

    decs, cross_grads = [], []
    for p in every:
        out = call(
            part(after_cross, p), (tgt_len,),
            [(full, BF16)] * 3 + [hid_spec] * 2 + [(full, BF16)] + blocks + [(full, F32), ((8, features), F32)],
            [(full, F32), (full, F32)], 7.0,
            *cross_mixes[p], firsts[p][0], *shares, *cross_shares, gains, biases, cgain, cbias, cotangent,
        )
        decs.append(out)
        cross_grads.append(exchange(out[6:10]))

    memory_total = ()
    query_grads, encoded_grads = [], []
    for p in every:
        out = call(
            part(cross_backward, p), lens,
            blocks + [((2,) + full, BF16)] * 2 + [((2, features, width), F32)],
            cross_scratch + back_spec, 8.0,
            *cross_grads[p], *cross_saved[p], *memories[p], memory_weights, *memory_total,
        )
        query_grads.append(exchange(out[:4]))
        encoded_grads.append(section_send(reduce_rows(out[4], out[5]).astype(BF16), 1))
        memory_total = (out[6],)
    memory_sent = section_send(memory_total[0].astype(BF16), 1)

    encs, self_grads = [], []
    for p in every:
        out = call(
            part(before_self, p), (),
            [(full, F32), (full, BF16)] + blocks + [(full, BF16), hid_spec, hid_spec, ((8, features), F32)],
            [(full, F32)], 6.0,
            firsts[p][0], firsts[p][1], firsts[p][2], gains, *shares, *cross_shares, encoded_grads[p],
            firsts[p][4], firsts[p][5], *query_grads[p], decs[p][10], decs[p][11],
        )
        encs.append(out)
        self_grads.append(exchange(out[2:6]))

    pair = lambda *tail: [((2,) + tail, BF16)] * 2
    up_even, up_odd, down_even, down_odd = call(
        part(ffn_grads, packs), (), pair(features, hidden) + pair(hidden, features), [], 5.0,
        *[d[1] for d in decs], *[d[3] for d in decs], *[d[2] for d in decs], *[d[4] for d in decs],
        *[f[2] for f in firsts], *[e[7] for e in encs], *[e[6] for e in encs], *[e[8] for e in encs],
    )
    out_even, out_odd, cross_even, cross_odd = call(
        part(projection_grads, packs), (), pair(width, features) + pair(2, features, width), [], 3.0,
        *sum(mixes, []), *[e[1] for e in encs],
        *sum(query_grads, []), *[f[2] for f in firsts],
        *sum(cross_mixes, []), *[d[5] for d in decs],
    )
    down_grad = chain_sum(reduce_rows(down_even, down_odd).astype(BF16))
    up_grad = chain_sum(reduce_rows(up_even, up_odd).astype(BF16))
    out_grad = chain_sum(reduce_rows(out_even, out_odd).astype(BF16))
    cross_own = reduce_rows(cross_even, cross_odd).astype(BF16)
    cross_grad = chain_sum(jnp.where(is_dec, cross_own, memory_sent))
    norms = tree_sum(sum(e[9] for e in encs))
    cross_norms = norms[4:6]
    cross_norms = jnp.where(is_dec, cross_norms, section_send(cross_norms, 1))

    qkv_total = ()
    input_grads = []
    for p in every:
        out = call(
            part(self_backward, p), lens,
            pair(rows, features) + [((3, features, width), F32)], self_scratch + back_spec, 8.0,
            *self_grads[p], *saved[p], *xs, w_self, *qkv_total,
        )
        input_grads.append(encs[p][0] + reduce_rows(out[0], out[1]))
        qkv_total = (out[2],)
    qkv_grad = chain_sum(qkv_total[0].astype(BF16))

    layer_rows = jnp.stack([jnp.where(is_dec, decs[p][0], firsts[p][3]) for p in every])
    wide = lambda value: value.astype(F32)[None]
    return (
        layer_rows[None],
        jnp.stack(input_grads)[None],
        wide(qkv_grad),
        wide(out_grad),
        wide(up_grad),
        wide(down_grad),
        wide(cross_grad[0]),
        wide(cross_grad[1]),
        norms[0:2][None],
        norms[2:4][None],
        cross_norms[0],
        cross_norms[1],
    )


def solution(mesh):
    return jax.shard_map(
        body,
        mesh=mesh,
        in_specs=(
            P("section", "dp", "mp", None),
            P("dp", None),
            P("dp", None),
            P("section", None, None, "mp"),
            P("section", "mp", None),
            P("section", None, "mp"),
            P("section", "mp", None),
            P("section", None, "mp"),
            P("section", None, "mp"),
            P("section", None, None),
            P("section", None, None),
            P(),
            P(),
            P("dp", "mp", None),
        ),
        out_specs=(
            P("section", "dp", "mp", None),
            P("section", "dp", "mp", None),
            P("section", None, None, "mp"),
            P("section", "mp", None),
            P("section", None, "mp"),
            P("section", "mp", None),
            P("section", None, "mp"),
            P("section", None, "mp"),
            P("section", None, None),
            P("section", None, None),
            P(),
            P(),
        ),
        check_vma=False,
    )
```

time: 2110 us -> 451 us (0.21)
  waiting for transfers between devices: 1130 us -> 208 us
  matrix products: 547 us -> 0 us
  other arithmetic: 201 us -> 13.2 us
  starting transfers between devices: 29.9 us -> 111 us
  blocking collectives: 77.6 us -> 0 us
  Pallas kernels: 0 us -> 76 us
  local copies, waits for them, and re-layouts: 89.5 us -> 30.2 us
    reduce_scatter x40 -> x0, waiting for transfers between devices: 750 us -> none  [narrow(): lax.psum_scatter(partial_value.astype(jnp.bfloat16), 'mp', scatter_dimens...]
    dot_general x237 -> x0, matrix products: 399 us -> none  [the longest x62 109 us: plain_dot(): return jnp.dot(left, right, preferred_element_type=jnp.float32)]
    all_gather x43 -> x0, waiting for transfers between devices: 340 us -> none  [widen(): return lax.all_gather(rows, 'mp', axis=0, tiled=True)]
    ppermute x12 -> x120, waiting for transfers between devices: 32.8 us -> 208 us  [the longest x94 106 us: hop(): return lax.ppermute(value, 'mp', [(i, i ^ distance) for i in range(count)])]
    sub x32 -> x0, matrix products: 148 us -> none  [softmax_block(): raised = jnp.exp(scores - top_score)]
    ppermute x12 -> x120, starting transfers between devices: 23.4 us -> 111 us  [the longest x94 61.7 us: hop(): return lax.ppermute(value, 'mp', [(i, i ^ distance) for i in range(count)])]
    psum x2 -> x0, blocking collectives: 77.6 us -> none  [the longest x1 42.6 us: body(): cross_total = lax.psum(cross_total, ('section', 'dp', 'mp'))]
    pallas_call x0 -> x23, Pallas kernels: none -> 76 us  [call(): pl.pallas_call(kernel, out_shape=[pltpu.VMEM(shape, kind) for shape, kind...]
  transfers between devices with their start and end apart: 96 -> 120, of which waited for: 73 -> 31; matrix products, arithmetic and copies ran while one was open for 32% -> 3% of each run, Pallas kernels for 0% -> 16%
where the time goes in v1:
time: 451 us; the launch traced here: 442 us
  waiting for transfers between devices  208 us (46%)
  starting transfers between devices  111 us (25%)
  Pallas kernels  76 us (17%)
  local copies, waits for them, and re-layouts  30.2 us (7%)
  other arithmetic  13.2 us (3%)
    ppermute x94, waiting for transfers between devices, hop(): return lax.ppermute(value, 'mp', [(i, i ^ distance) for i in range(count)])  106 us
    pallas_call x23, Pallas kernels, call(): pl.pallas_call(kernel, out_shape=[pltpu.VMEM(shape, kind) for shape, kind...  76 us
    ppermute x94, starting transfers between devices, hop(): return lax.ppermute(value, 'mp', [(i, i ^ distance) for i in range(count)])  61.7 us
    ppermute x9, waiting for transfers between devices, section_send(): return lax.ppermute(value, 'section', [(source, 1 - source)])  53.4 us
    ppermute x5, waiting for transfers between devices, chain_sum(): lax.ppermute(values, 'dp', [(i + 1, i), (count - 2 - i, count - 1 - i)])  35.5 us
    unnamed x260, local copies, waits for them, and re-layouts  29.7 us
    ppermute x5, starting transfers between devices, chain_sum(): lax.ppermute(values, 'dp', [(i, i + 1), (count - 1 - i, count - 2 - i)])  18.9 us
    ppermute x9, starting transfers between devices, section_send(): return lax.ppermute(value, 'section', [(source, 1 - source)])  15.8 us
  transfers between devices with their start and end apart: 120, of which 31 were waited for; matrix products, arithmetic and copies ran while one was open for 3% of the time, Pallas kernels for 16%

profile of v1, /device:TPU:0, one launch (start us, length us, event | category | flops | bytes accessed | tf_op | source)
XLA Modules:
  0.0 441.7 jit_solution(9317556396846888275)
XLA Ops:
  3.7 17.7 %collective-permute-done.1.x2 = bf16[3,256,512]{2,1,0:T(8,128)(2,1)S(1)} collective-permute-done((bf16[3,256,512]{2,1,0:T(8,128)(2,1)}, bf16[3,256,512]{2,1,0:T(8,128)(2,1)S(1)}, u32[]{:S(2)}, u32[]{:S(2)}) %collective-permute-start.1) | collective-permute-done | bytes 786464 | tf_op jit(solution)/shard_map/ppermute | solution.py:32
  25.9 26.4 %collective-permute-done.7.w2 = bf16[1152,512]{1,0:T(8,128)(2,1)S(1)} collective-permute-done((bf16[1152,512]{1,0:T(8,128)(2,1)S(1)}, bf16[1152,512]{1,0:T(8,128)(2,1)S(1)}, u32[]{:S(2)}, u32[]{:S(2)}) %collective-permute-start.7) | collective-permute-done | bytes 1179680 | tf_op jit(solution)/shard_map/ppermute | solution.py:32
  52.3 6.3 %shard_map.229 = (bf16[256,128]{1,0:T(8,128)(2,1)S(1)}, bf16[256,128]{1,0:T(8,128)(2,1)S(1)}, bf16[256,128]{1,0:T(8,128)(2,1)S(1)}, bf16[256,128]{1,0:T(8,128)(2...) custom-call(s32[3,4]{1,0:T(4,128)S(1)} %copy-done.57, ...), custom_call_target="tpu_custom_call" | custom-call | flops 5000000000 | bytes 65536 | tf_op jit(solution)/shard_map/pallas_call | solution.py:613
  64.7 6.3 %shard_map.233 = (bf16[256,128]{1,0:T(8,128)(2,1)S(1)}, bf16[256,128]{1,0:T(8,128)(2,1)S(1)}, bf16[256,128]{1,0:T(8,128)(2,1)S(1)}, bf16[256,128]{1,0:T(8,128)(2...) custom-call(s32[3,4]{1,0:T(4,128)S(1)} %copy-done.57, ...), custom_call_target="tpu_custom_call" | custom-call | flops 5000000000 | bytes 65536 | tf_op jit(solution)/shard_map/pallas_call | solution.py:613
  76.5 6.3 %shard_map.237 = (bf16[256,128]{1,0:T(8,128)(2,1)S(1)}, bf16[256,128]{1,0:T(8,128)(2,1)S(1)}, bf16[256,128]{1,0:T(8,128)(2,1)S(1)}, bf16[256,128]{1,0:T(8,128)(2...) custom-call(s32[3,4]{1,0:T(4,128)S(1)} %copy-done.57, ...), custom_call_target="tpu_custom_call" | custom-call | flops 5000000000 | bytes 65536 | tf_op jit(solution)/shard_map/pallas_call | solution.py:613
  83.7 3.4 collective-permute-start.19
  99.9 3.5 shard_map.234
  125.4 7.5 %collective-permute-done.13.q2 = bf16[256,128]{1,0:T(8,128)(2,1)S(1)} collective-permute-done((bf16[256,128]{1,0:T(8,128)(2,1)S(1)}, bf16[256,128]{1,0:T(8,128)(2,1)S(1)}, u32[]{:S(2)}, u32[]{:S(2)}) %collective-permute-start.13) | collective-permute-done | bytes 65568 | tf_op jit(solution)/shard_map/ppermute | solution.py:32
  134.3 3.5 collective-permute-done.14.q3
  176.5 4.3 shard_map.247
  185.3 7.6 %collective-permute-done.53 = bf16[256,512]{1,0:T(8,128)(2,1)S(1)} collective-permute-done((bf16[256,512]{1,0:T(8,128)(2,1)S(1)}, bf16[256,512]{1,0:T(8,128)(2,1)S(1)}, u32[]{:S(2)}, u32[]{:S(2)}) %collective-permute-start.53) | collective-permute-done | bytes 262176 | tf_op jit(solution)/shard_map/ppermute | solution.py:32
  194.3 4.2 collective-permute-done.67
  199.9 4.0 collective-permute-done.81
  206.3 47.2 %collective-permute-done.54.grad_encoded = bf16[256,512]{1,0:T(8,128)(2,1)S(1)} collective-permute-done((bf16[256,512]{1,0:T(8,128)(2,1)S(1)}, bf16[256,512]{1,0:T(8,128)(2,1)S(1)}, u32[]{:S(2)}, u32[]{:S(2)}) %collective-permute-start.54) | collective-permute-done | bytes 262176 | tf_op jit(solution)/shard_map/ppermute | solution.py:51
  265.4 4.0 collective-permute-done.82.grad_encoded
  281.6 3.5 shard_map.251
  292.0 7.3 %shard_map.243 = (bf16[2,256,512]{2,1,0:T(8,128)(2,1)S(1)}, bf16[2,256,512]{2,1,0:T(8,128)(2,1)S(1)}, f32[3,512,128]{2,1,0:T(8,128)S(1)}) custom-call(s32[3,4]{1,0:T(4,128)S(1)} %copy-done.57, s32[3,4]{1,0:T(4,128)S(1)} %copy-done.56, bf16[256,128]{1,0:T(8,128)(2,1)S(1)} %get-tuple-element.279.g0, bf16[256,128]{1,0:T(8,128)(2,1)S(1)} %collective-permute-done.58.g1, ...), custom_call_target="tpu_custom_call" | custom-call | flops 8000000000 | bytes 65536 | tf_op jit(solution)/shard_map/pallas_call | solution.py:613
  301.5 7.3 %shard_map.246 = (bf16[2,256,512]{2,1,0:T(8,128)(2,1)S(1)}, bf16[2,256,512]{2,1,0:T(8,128)(2,1)S(1)}, f32[3,512,128]{2,1,0:T(8,128)S(1)}) custom-call(s32[3,4]{1,0:T(4,128)S(1)} %copy-done.57, s32[3,4]{1,0:T(4,128)S(1)} %copy-done.56, bf16[256,128]{1,0:T(8,128)(2,1)S(1)} %get-tuple-element.313.g0, bf16[256,128]{1,0:T(8,128)(2,1)S(1)} %collective-permute-done.72.g1, ...), custom_call_target="tpu_custom_call" | custom-call | flops 8000000000 | bytes 65536 | tf_op jit(solution)/shard_map/pallas_call | solution.py:613
  311.0 7.3 %shard_map.249 = (bf16[2,256,512]{2,1,0:T(8,128)(2,1)S(1)}, bf16[2,256,512]{2,1,0:T(8,128)(2,1)S(1)}, f32[3,512,128]{2,1,0:T(8,128)S(1)}) custom-call(s32[3,4]{1,0:T(4,128)S(1)} %copy-done.57, s32[3,4]{1,0:T(4,128)S(1)} %copy-done.56, bf16[256,128]{1,0:T(8,128)(2,1)S(1)} %get-tuple-element.348.g0, bf16[256,128]{1,0:T(8,128)(2,1)S(1)} %collective-permute-done.86.g1, ...), custom_call_target="tpu_custom_call" | custom-call | flops 8000000000 | bytes 65536 | tf_op jit(solution)/shard_map/pallas_call | solution.py:613
  322.5 4.5 %collective-permute-done.95 = bf16[128,512]{1,0:T(8,128)(2,1)S(1)} collective-permute-done((bf16[128,512]{1,0:T(8,128)(2,1)S(1)}, bf16[128,512]{1,0:T(8,128)(2,1)S(1)}, u32[]{:S(2)}, u32[]{:S(2)}) %collective-permute-start.95) | collective-permute-done | bytes 131104 | tf_op jit(solution)/shard_map/ppermute | solution.py:32
  329.7 4.4 collective-permute-start.96
  342.2 5.2 %collective-permute-done.110 = bf16[2,512,128]{2,1,0:T(8,128)(2,1)S(1)} collective-permute-done((bf16[2,512,128]{2,1,0:T(8,128)(2,1)S(1)}, bf16[2,512,128]{2,1,0:T(8,128)(2,1)S(1)}, u32[]{:S(2)}, u32[]{:S(2)}) %collective-permute-start.110) | collective-permute-done | bytes 262176 | tf_op jit(solution)/shard_map/ppermute | solution.py:32
  348.9 9.9 %collective-permute-done.98 = bf16[128,512]{1,0:T(8,128)(2,1)S(1)} collective-permute-done((bf16[128,512]{1,0:T(8,128)(2,1)S(1)}, bf16[128,512]{1,0:T(8,128)(2,1)S(1)}, u32[]{:S(2)}, u32[]{:S(2)}) %collective-permute-start.98) | collective-permute-done | bytes 131104 | tf_op jit(solution)/shard_map/ppermute | solution.py:68
  361.8 3.6 collective-permute-start.112
  373.1 11.1 %collective-permute-done.105 = bf16[512,512]{1,0:T(8,128)(2,1)S(1)} collective-permute-done((bf16[512,512]{1,0:T(8,128)(2,1)S(1)}, bf16[512,512]{1,0:T(8,128)(2,1)S(1)}, u32[]{:S(2)}, u32[]{:S(2)}) %collective-permute-start.105) | collective-permute-done | bytes 524320 | tf_op jit(solution)/shard_map/ppermute | solution.py:32
  384.4 4.4 %collective-permute-start.106 = (bf16[512,512]{1,0:T(8,128)(2,1)S(1)}, bf16[512,512]{1,0:T(8,128)(2,1)S(1)}, u32[]{:S(2)}, u32[]{:S(2)}) collective-permute-start(bf16[512,512]{1,0:T(8,128)(2,1)S(1)} %fusion), channel_id=1, source_target_pairs={{0,4},{12,8},{1,5},{13,9},{2,6},{14,10},{3,7},{15,11},{16,20},{28,... | collective-permute-start | bytes 1572872 | tf_op jit(solution)/shard_map/ppermute | solution.py:62
  388.9 3.9 collective-permute-done.100
  393.0 4.2 collective-permute-start.101
  400.1 6.7 %collective-permute-done.101 = bf16[512,512]{1,0:T(8,128)(2,1)S(1)} collective-permute-done((bf16[512,512]{1,0:T(8,128)(2,1)S(1)}, bf16[512,512]{1,0:T(8,128)(2,1)S(1)}, u32[]{:S(2)}, u32[]{:S(2)}) %collective-permute-start.101) | collective-permute-done | bytes 524320 | tf_op jit(solution)/shard_map/ppermute | solution.py:62
  412.8 8.5 %collective-permute-done.114 = bf16[2,512,128]{2,1,0:T(8,128)(2,1)S(1)} collective-permute-done((bf16[2,512,128]{2,1,0:T(8,128)(2,1)S(1)}, bf16[2,512,128]{2,1,0:T(8,128)(2,1)S(1)}, u32[]{:S(2)}, u32[]{:S(2)}) %collective-permute-start.114) | collective-permute-done | bytes 262176 | tf_op jit(solution)/shard_map/ppermute | solution.py:68
  422.1 9.6 %collective-permute-done.108 = bf16[512,512]{1,0:T(8,128)(2,1)S(1)} collective-permute-done((bf16[512,512]{1,0:T(8,128)(2,1)S(1)}, bf16[512,512]{1,0:T(8,128)(2,1)S(1)}, u32[]{:S(2)}, u32[]{:S(2)}) %collective-permute-start.108) | collective-permute-done | bytes 524320 | tf_op jit(solution)/shard_map/ppermute | solution.py:68
  432.8 7.4 %collective-permute-done.103 = bf16[512,512]{1,0:T(8,128)(2,1)S(1)} collective-permute-done((bf16[512,512]{1,0:T(8,128)(2,1)S(1)}, bf16[512,512]{1,0:T(8,128)(2,1)S(1)}, u32[]{:S(2)}, u32[]{:S(2)}) %collective-permute-start.103) | collective-permute-done | bytes 524320 | tf_op jit(solution)/shard_map/ppermute | solution.py:68
  (544 shorter events, 177.7 us)
Async XLA Ops:
  0.7 20.8 %collective-permute-start.1 = (bf16[3,256,512]{2,1,0:T(8,128)(2,1)}, bf16[3,256,512]{2,1,0:T(8,128)(2,1)S(1)}, u32[]{:S(2)}, u32[]{:S(2)}) collective-permute-start(bf16[3,256,512]{2,1,0:T(8,128)(2,1)} %bitcast.111), channel_id=1, source_target_pairs={{0,2},{1,3},{2,0},{3,1},{4,6},{5,7},{6,4},{7,5},{8,10},{9,11},{10,... | collective-permute-start | bytes 2359304 | tf_op jit(solution)/shard_map/ppermute | solution.py:32
  3.7 20.3 %collective-permute-start = (bf16[3,256,512]{2,1,0:T(8,128)(2,1)}, bf16[3,256,512]{2,1,0:T(8,128)(2,1)S(1)}, u32[]{:S(2)}, u32[]{:S(2)}) collective-permute-start(bf16[3,256,512]{2,1,0:T(8,128)(2,1)} %bitcast.112), channel_id=1, source_target_pairs={{0,1},{1,0},{2,3},{3,2},{4,5},{5,4},{6,7},{7,6},{8,9},{9,8},{10,11... | collective-permute-start | bytes 2359304 | tf_op jit(solution)/shard_map/ppermute | solution.py:32
  24.1 28.2 %collective-permute-start.7 = (bf16[1152,512]{1,0:T(8,128)(2,1)S(1)}, bf16[1152,512]{1,0:T(8,128)(2,1)S(1)}, u32[]{:S(2)}, u32[]{:S(2)}) collective-permute-start(bf16[1152,512]{1,0:T(8,128)(2,1)S(1)} %pad_maximum_fusion.w0), channel_id=1, source_target_pairs={{0,2},{1,3},{2,0},{3,1},{4,6},{5,7},{6,4},{7,5},{8,10},{9,11},{10,... | collective-permute-start | bytes 3538952 | tf_op jit(solution)/shard_map/ppermute | solution.py:32
  25.9 61.9 %collective-permute-start.6 = (bf16[1152,512]{1,0:T(8,128)(2,1)S(1)}, bf16[1152,512]{1,0:T(8,128)(2,1)S(1)}, u32[]{:S(2)}, u32[]{:S(2)}) collective-permute-start(bf16[1152,512]{1,0:T(8,128)(2,1)S(1)} %pad_maximum_fusion.w0), channel_id=1, source_target_pairs={{0,1},{1,0},{2,3},{3,2},{4,5},{5,4},{6,7},{7,6},{8,9},{9,8},{10,11... | collective-permute-start | bytes 3538952 | tf_op jit(solution)/shard_map/ppermute | solution.py:32
  52.3 36.8 %collective-permute-start.8 = (bf16[1152,512]{1,0:T(8,128)(2,1)S(1)}, bf16[1152,512]{1,0:T(8,128)(2,1)S(1)}, u32[]{:S(2)}, u32[]{:S(2)}) collective-permute-start(bf16[1152,512]{1,0:T(8,128)(2,1)S(1)} %collective-permute-done.7.w2), channel_id=1, source_target_pairs={{0,1},{1,0},{2,3},{3,2},{4,5},{5,4},{6,7},{7,6},{8,9},{9,8},{10,11... | collective-permute-start | bytes 3538952 | tf_op jit(solution)/shard_map/ppermute | solution.py:32
  83.7 38.2 %collective-permute-start.19 = (bf16[2,512,128]{2,1,0:T(8,128)(2,1)S(1)}, bf16[2,512,128]{2,1,0:T(8,128)(2,1)S(1)}, u32[]{:S(2)}, u32[]{:S(2)}) collective-permute-start(bf16[2,512,128]{2,1,0:T(8,128)(2,1)S(1)} %pad_maximum_fusion.1.k0), channel_id=1, source_target_pairs={{0,16},{1,17},{2,18},{3,19},{4,20},{5,21},{6,22},{7,23},{8,24},{9,... | collective-permute-start | bytes 786440 | tf_op jit(solution)/shard_map/ppermute | solution.py:51
  89.0 18.6 %collective-permute-start.36 = (bf16[256,128]{1,0:T(8,128)(2,1)S(1)}, bf16[256,128]{1,0:T(8,128)(2,1)S(1)}, u32[]{:S(2)}, u32[]{:S(2)}) collective-permute-start(bf16[256,128]{1,0:T(8,128)(2,1)S(1)} %get-tuple-element.243), channel_id=1, source_target_pairs={{0,1},{1,0},{2,3},{3,2},{4,5},{5,4},{6,7},{7,6},{8,9},{9,8},{10,11... | collective-permute-start | bytes 196616 | tf_op jit(solution)/shard_map/ppermute | solution.py:32
  107.6 16.7 %collective-permute-start.12 = (bf16[256,128]{1,0:T(8,128)(2,1)S(1)}, bf16[256,128]{1,0:T(8,128)(2,1)S(1)}, u32[]{:S(2)}, u32[]{:S(2)}) collective-permute-start(bf16[256,128]{1,0:T(8,128)(2,1)S(1)} %get-tuple-element.217), channel_id=1, source_target_pairs={{0,1},{1,0},{2,3},{3,2},{4,5},{5,4},{6,7},{7,6},{8,9},{9,8},{10,11... | collective-permute-start | bytes 196616 | tf_op jit(solution)/shard_map/ppermute | solution.py:32
  119.8 21.7 %collective-permute-start.42 = (bf16[256,512]{1,0:T(8,128)(2,1)S(1)}, bf16[256,512]{1,0:T(8,128)(2,1)}, u32[]{:S(2)}, u32[]{:S(2)}) collective-permute-start(bf16[256,512]{1,0:T(8,128)(2,1)S(1)} %get-tuple-element.250), channel_id=1, source_target_pairs={{0,16},{1,17},{2,18},{3,19},{4,20},{5,21},{6,22},{7,23},{8,24},{9,... | collective-permute-start | bytes 786440 | tf_op jit(solution)/shard_map/ppermute | solution.py:51
  122.5 19.0 %collective-permute-start.16 = (bf16[256,512]{1,0:T(8,128)(2,1)}, bf16[256,512]{1,0:T(8,128)(2,1)}, u32[]{:S(2)}, u32[]{:S(2)}) collective-permute-start(bf16[256,512]{1,0:T(8,128)(2,1)} %collective-permute-done.15.e0), channel_id=1, source_target_pairs={{0,1},{1,0},{2,3},{3,2},{4,5},{5,4},{6,7},{7,6},{8,9},{9,8},{10,11... | collective-permute-start | bytes 786440 | tf_op jit(solution)/shard_map/ppermute | solution.py:32
  122.5 19.6 %collective-permute-start.31 = (bf16[256,512]{1,0:T(8,128)(2,1)}, bf16[256,512]{1,0:T(8,128)(2,1)}, u32[]{:S(2)}, u32[]{:S(2)}) collective-permute-start(bf16[256,512]{1,0:T(8,128)(2,1)} %collective-permute-done.29.e0), channel_id=1, source_target_pairs={{0,2},{1,3},{2,0},{3,1},{4,6},{5,7},{6,4},{7,5},{8,10},{9,11},{10,... | collective-permute-start | bytes 786440 | tf_op jit(solution)/shard_map/ppermute | solution.py:32
  124.1 19.6 %collective-permute-start.18 = (bf16[256,512]{1,0:T(8,128)(2,1)}, bf16[256,512]{1,0:T(8,128)(2,1)}, u32[]{:S(2)}, u32[]{:S(2)}) collective-permute-start(bf16[256,512]{1,0:T(8,128)(2,1)} %collective-permute-done.17.e2), channel_id=1, source_target_pairs={{0,1},{1,0},{2,3},{3,2},{4,5},{5,4},{6,7},{7,6},{8,9},{9,8},{10,11... | collective-permute-start | bytes 786440 | tf_op jit(solution)/shard_map/ppermute | solution.py:32
  180.9 23.2 %collective-permute-start.55 = (bf16[256,128]{1,0:T(8,128)(2,1)S(1)}, bf16[256,128]{1,0:T(8,128)(2,1)S(1)}, u32[]{:S(2)}, u32[]{:S(2)}) collective-permute-start(bf16[256,128]{1,0:T(8,128)(2,1)S(1)} %get-tuple-element.273), channel_id=1, source_target_pairs={{0,1},{1,0},{2,3},{3,2},{4,5},{5,4},{6,7},{7,6},{8,9},{9,8},{10,11... | collective-permute-start | bytes 196616 | tf_op jit(solution)/shard_map/ppermute | solution.py:32
  181.4 23.8 %collective-permute-start.56 = (bf16[256,128]{1,0:T(8,128)(2,1)S(1)}, bf16[256,128]{1,0:T(8,128)(2,1)S(1)}, u32[]{:S(2)}, u32[]{:S(2)}) collective-permute-start(bf16[256,128]{1,0:T(8,128)(2,1)S(1)} %get-tuple-element.274), channel_id=1, source_target_pairs={{0,2},{1,3},{2,0},{3,1},{4,6},{5,7},{6,4},{7,5},{8,10},{9,11},{10,... | collective-permute-start | bytes 196616 | tf_op jit(solution)/shard_map/ppermute | solution.py:32
  182.6 23.4 %collective-permute-start.57 = (bf16[256,128]{1,0:T(8,128)(2,1)S(1)}, bf16[256,128]{1,0:T(8,128)(2,1)S(1)}, u32[]{:S(2)}, u32[]{:S(2)}) collective-permute-start(bf16[256,128]{1,0:T(8,128)(2,1)S(1)} %get-tuple-element.275), channel_id=1, source_target_pairs={{0,3},{1,2},{2,1},{3,0},{4,7},{5,6},{6,5},{7,4},{8,11},{9,10},{10,... | collective-permute-start | bytes 196616 | tf_op jit(solution)/shard_map/ppermute | solution.py:32
  198.5 55.0 %collective-permute-start.54 = (bf16[256,512]{1,0:T(8,128)(2,1)S(1)}, bf16[256,512]{1,0:T(8,128)(2,1)S(1)}, u32[]{:S(2)}, u32[]{:S(2)}) collective-permute-start(bf16[256,512]{1,0:T(8,128)(2,1)S(1)} %fusion.13), channel_id=1, source_target_pairs={{16,0},{17,1},{18,2},{19,3},{20,4},{21,5},{22,6},{23,7},{24,8},{25... | collective-permute-start | bytes 786440 | tf_op jit(solution)/shard_map/ppermute | solution.py:51
  203.9 54.1 %collective-permute-start.69 = (bf16[256,128]{1,0:T(8,128)(2,1)S(1)}, bf16[256,128]{1,0:T(8,128)(2,1)S(1)}, u32[]{:S(2)}, u32[]{:S(2)}) collective-permute-start(bf16[256,128]{1,0:T(8,128)(2,1)S(1)} %get-tuple-element.307), channel_id=1, source_target_pairs={{0,1},{1,0},{2,3},{3,2},{4,5},{5,4},{6,7},{7,6},{8,9},{9,8},{10,11... | collective-permute-start | bytes 196616 | tf_op jit(solution)/shard_map/ppermute | solution.py:32
  204.1 54.7 %collective-permute-start.70 = (bf16[256,128]{1,0:T(8,128)(2,1)S(1)}, bf16[256,128]{1,0:T(8,128)(2,1)S(1)}, u32[]{:S(2)}, u32[]{:S(2)}) collective-permute-start(bf16[256,128]{1,0:T(8,128)(2,1)S(1)} %get-tuple-element.308), channel_id=1, source_target_pairs={{0,2},{1,3},{2,0},{3,1},{4,6},{5,7},{6,4},{7,5},{8,10},{9,11},{10,... | collective-permute-start | bytes 196616 | tf_op jit(solution)/shard_map/ppermute | solution.py:32
  205.3 53.5 %collective-permute-start.71 = (bf16[256,128]{1,0:T(8,128)(2,1)S(1)}, bf16[256,128]{1,0:T(8,128)(2,1)S(1)}, u32[]{:S(2)}, u32[]{:S(2)}) collective-permute-start(bf16[256,128]{1,0:T(8,128)(2,1)S(1)} %get-tuple-element.309), channel_id=1, source_target_pairs={{0,3},{1,2},{2,1},{3,0},{4,7},{5,6},{6,5},{7,4},{8,11},{9,10},{10,... | collective-permute-start | bytes 196616 | tf_op jit(solution)/shard_map/ppermute | solution.py:32
  206.0 59.4 %collective-permute-start.83 = (bf16[256,128]{1,0:T(8,128)(2,1)S(1)}, bf16[256,128]{1,0:T(8,128)(2,1)S(1)}, u32[]{:S(2)}, u32[]{:S(2)}) collective-permute-start(bf16[256,128]{1,0:T(8,128)(2,1)S(1)} %get-tuple-element.342), channel_id=1, source_target_pairs={{0,1},{1,0},{2,3},{3,2},{4,5},{5,4},{6,7},{7,6},{8,9},{9,8},{10,11... | collective-permute-start | bytes 196616 | tf_op jit(solution)/shard_map/ppermute | solution.py:32
  276.6 64.6 %collective-permute-start.111 = (bf16[2,512,128]{2,1,0:T(8,128)(2,1)S(1)}, bf16[2,512,128]{2,1,0:T(8,128)(2,1)S(1)}, u32[]{:S(2)}, u32[]{:S(2)}) collective-permute-start(bf16[2,512,128]{2,1,0:T(8,128)(2,1)S(1)} %convert_element_type.481), channel_id=1, source_target_pairs={{16,0},{17,1},{18,2},{19,3},{20,4},{21,5},{22,6},{23,7},{24,8},{25... | collective-permute-start | bytes 786440 | tf_op jit(solution)/shard_map/ppermute | solution.py:51
  289.8 39.9 %collective-permute-start.109 = (bf16[2,2,512,128]{3,2,1,0:T(8,128)(2,1)S(1)}, bf16[2,2,512,128]{3,2,1,0:T(8,128)(2,1)S(1)}, u32[]{:S(2)}, u32[]{:S(2)}) collective-permute-start(bf16[2,2,512,128]{3,2,1,0:T(8,128)(2,1)S(1)} %get-tuple-element.395), channel_id=1, source_target_pairs={{0,1},{1,0},{2,3},{3,2},{4,5},{5,4},{6,7},{7,6},{8,9},{9,8},{10,11... | collective-permute-start | bytes 1572872 | tf_op jit(solution)/shard_map/ppermute | solution.py:32
  308.8 60.1 %collective-permute-start.104 = (bf16[2,512,512]{2,1,0:T(8,128)(2,1)S(1)}, bf16[2,512,512]{2,1,0:T(8,128)(2,1)S(1)}, u32[]{:S(2)}, u32[]{:S(2)}) collective-permute-start(bf16[2,512,512]{2,1,0:T(8,128)(2,1)S(1)} %get-tuple-element.393), channel_id=1, source_target_pairs={{0,1},{1,0},{2,3},{3,2},{4,5},{5,4},{6,7},{7,6},{8,9},{9,8},{10,11... | collective-permute-start | bytes 3145736 | tf_op jit(solution)/shard_map/ppermute | solution.py:32
  337.6 33.6 %collective-permute-start.99 = (bf16[2,512,512]{2,1,0:T(8,128)(2,1)S(1)}, bf16[2,512,512]{2,1,0:T(8,128)(2,1)S(1)}, u32[]{:S(2)}, u32[]{:S(2)}) collective-permute-start(bf16[2,512,512]{2,1,0:T(8,128)(2,1)S(1)} %get-tuple-element.391), channel_id=1, source_target_pairs={{0,1},{1,0},{2,3},{3,2},{4,5},{5,4},{6,7},{7,6},{8,9},{9,8},{10,11... | collective-permute-start | bytes 3145736 | tf_op jit(solution)/shard_map/ppermute | solution.py:32
  340.4 21.3 %collective-permute-start.92 = (bf16[3,512,128]{2,1,0:T(8,128)(2,1)S(1)}, bf16[3,512,128]{2,1,0:T(8,128)(2,1)S(1)}, u32[]{:S(2)}, u32[]{:S(2)}) collective-permute-start(bf16[3,512,128]{2,1,0:T(8,128)(2,1)S(1)} %add_convert_fusion.7), channel_id=1, source_target_pairs={{4,8},{8,4},{5,9},{9,5},{6,10},{10,6},{7,11},{11,7},{20,24},{24,20... | collective-permute-start | bytes 1179656 | tf_op jit(solution)/shard_map/ppermute | solution.py:65
  341.2 19.8 %collective-permute-start.62 = (bf16[256,512]{1,0:T(8,128)(2,1)S(1)}, bf16[256,512]{1,0:T(8,128)(2,1)S(1)}, u32[]{:S(2)}, u32[]{:S(2)}) collective-permute-start(bf16[256,512]{1,0:T(8,128)(2,1)S(1)} %fusion.15), channel_id=1, source_target_pairs={{0,2},{1,3},{2,0},{3,1},{4,6},{5,7},{6,4},{7,5},{8,10},{9,11},{10,... | collective-permute-start | bytes 786440 | tf_op jit(solution)/shard_map/ppermute | solution.py:32
  361.8 36.7 %collective-permute-start.112 = (bf16[2,512,128]{2,1,0:T(8,128)(2,1)S(1)}, bf16[2,512,128]{2,1,0:T(8,128)(2,1)S(1)}, u32[]{:S(2)}, u32[]{:S(2)}) collective-permute-start(bf16[2,512,128]{2,1,0:T(8,128)(2,1)S(1)} %fusion.21), channel_id=1, source_target_pairs={{0,4},{12,8},{1,5},{13,9},{2,6},{14,10},{3,7},{15,11},{16,20},{28,... | collective-permute-start | bytes 786440 | tf_op jit(solution)/shard_map/ppermute | solution.py:62
  367.5 40.1 %collective-permute-start.93 = (bf16[3,512,128]{2,1,0:T(8,128)(2,1)S(1)}, bf16[3,512,128]{2,1,0:T(8,128)(2,1)S(1)}, u32[]{:S(2)}, u32[]{:S(2)}) collective-permute-start(bf16[3,512,128]{2,1,0:T(8,128)(2,1)S(1)} %add_convert_fusion.6), channel_id=1, source_target_pairs={{4,0},{8,12},{5,1},{9,13},{6,2},{10,14},{7,3},{11,15},{20,16},{24,... | collective-permute-start | bytes 1179656 | tf_op jit(solution)/shard_map/ppermute | solution.py:68
  369.1 15.1 %collective-permute-start.105 = (bf16[512,512]{1,0:T(8,128)(2,1)S(1)}, bf16[512,512]{1,0:T(8,128)(2,1)S(1)}, u32[]{:S(2)}, u32[]{:S(2)}) collective-permute-start(bf16[512,512]{1,0:T(8,128)(2,1)S(1)} %fusion.3), channel_id=1, source_target_pairs={{0,2},{1,3},{2,0},{3,1},{4,6},{5,7},{6,4},{7,5},{8,10},{9,11},{10,... | collective-permute-start | bytes 1572872 | tf_op jit(solution)/shard_map/ppermute | solution.py:32
  371.3 21.4 %collective-permute-start.100 = (bf16[512,512]{1,0:T(8,128)(2,1)S(1)}, bf16[512,512]{1,0:T(8,128)(2,1)S(1)}, u32[]{:S(2)}, u32[]{:S(2)}) collective-permute-start(bf16[512,512]{1,0:T(8,128)(2,1)S(1)} %fusion.2), channel_id=1, source_target_pairs={{0,2},{1,3},{2,0},{3,1},{4,6},{5,7},{6,4},{7,5},{8,10},{9,11},{10,... | collective-permute-start | bytes 1572872 | tf_op jit(solution)/shard_map/ppermute | solution.py:32
  410.1 21.7 %collective-permute-start.108 = (bf16[512,512]{1,0:T(8,128)(2,1)S(1)}, bf16[512,512]{1,0:T(8,128)(2,1)S(1)}, u32[]{:S(2)}, u32[]{:S(2)}) collective-permute-start(bf16[512,512]{1,0:T(8,128)(2,1)S(1)} %add_convert_fusion), channel_id=1, source_target_pairs={{4,0},{8,12},{5,1},{9,13},{6,2},{10,14},{7,3},{11,15},{20,16},{24,... | collective-permute-start | bytes 1572872 | tf_op jit(solution)/shard_map/ppermute | solution.py:68
  411.5 28.7 %collective-permute-start.103 = (bf16[512,512]{1,0:T(8,128)(2,1)S(1)}, bf16[512,512]{1,0:T(8,128)(2,1)S(1)}, u32[]{:S(2)}, u32[]{:S(2)}) collective-permute-start(bf16[512,512]{1,0:T(8,128)(2,1)S(1)} %add_convert_fusion.3), channel_id=1, source_target_pairs={{4,0},{8,12},{5,1},{9,13},{6,2},{10,14},{7,3},{11,15},{20,16},{24,... | collective-permute-start | bytes 1572872 | tf_op jit(solution)/shard_map/ppermute | solution.py:68
  (218 other events, 2033.6 us)
